TPU v7x, 256 devices: a whole 4x4x8 slice. The times are simulated.
256 devices in a mesh: tensor: 8 (over z), sibling: 16 (over y, x), replica: 2 (over core).
Axes of the slice: x: 4, y: 4, z: 8, core: 2. Of those that a mesh axis runs over, the one named last changes fastest.
Arguments:
- reply_x: bfloat16 [512, 8, 16384], P(('replica', 'sibling'), None, 'tensor'), parts along dimension 0, may hold values from -6 to 6
- reply_bc: bfloat16 [512, 8, 2, 2048], P(('replica', 'sibling'), None, None, 'tensor'), parts along dimension 0, may hold values from -6 to 6
- reply_dt: bfloat16 [512, 8, 256], P(('replica', 'sibling'), None, 'tensor'), parts along dimension 0, may hold values from -4 to 4
- reply_gate: bfloat16 [512, 8, 16384], P(('replica', 'sibling'), None, 'tensor'), parts along dimension 0, may hold values from -6 to 6
- reply_query: bfloat16 [512, 8, 8192], P(('replica', 'sibling'), None, 'tensor'), parts along dimension 0, may hold values from -40 to 40
- reply_kv: bfloat16 [512, 8, 2, 1024], P(('replica', 'sibling'), None, None, 'tensor'), parts along dimension 0, may hold values from -21 to 21
- lengths: int32 [512], P(('replica', 'sibling')), parts along dimension 0, may hold values from 1 to 8, 1280 in all
- fork_list: int32 [512, 1], P(('replica', 'sibling')), parts along dimension 0, may hold values from 0 to 15; in each aligned block of 16 rows (0 to 15, 16 to 31, ...) at most 2 rows name the same one
- ssm_state: float32 [32, 256, 64, 256], P(('replica', 'sibling'), 'tensor'), parts along dimension 0, may hold values from -1.2 to 1.2
- conv_x: bfloat16 [32, 3, 16384], P(('replica', 'sibling'), None, 'tensor'), parts along dimension 0, may hold values from -6 to 6
- conv_bc: bfloat16 [32, 3, 2, 2048], P(('replica', 'sibling'), None, None, 'tensor'), parts along dimension 0, may hold values from -6 to 6
- kv_pool: bfloat16 [1024, 128, 2, 1024], P(('replica', 'sibling'), None, None, 'tensor'), parts along dimension 0, may hold values from -16 to 16
- page_table: int32 [32, 16], P(('replica', 'sibling')), parts along dimension 0, may hold values from 0 to 31, as said below
- kernel_x: float32 [4, 16384], P(None, 'tensor'), may hold values from -2.5 to 2.5
- kernel_bc: float32 [4, 2, 2048], P(None, None, 'tensor'), may hold values from -2.5 to 2.5
- a_log: float32 [256], P('tensor'), may hold values from -1 to 1.5
- dt_bias: float32 [256], P('tensor'), may hold values from -4 to 0
- d_skip: float32 [256], P('tensor'), may hold values from 0.5 to 2
- norm_gain: float32 [16384], P('tensor'), may hold values from 0.1 to 1.9
Outputs:
- mamba_out: bfloat16 [512, 8, 16384], P(('replica', 'sibling'), None, 'tensor'), parts along dimension 0
- attn_out: bfloat16 [512, 8, 8192], P(('replica', 'sibling'), None, 'tensor'), parts along dimension 0
There are 2 independent parts, one for each index of `replica`. A program takes and returns all parts, laid end to end along the dimension named above; an argument that names none is the same for every part. Nothing has to cross between parts.
Inputs may be any that keep to these rules, and one draw needn't show every extreme that they name: fork_list[c, 0] is the parent of child c. Among the 16 children of one device (aligned blocks of rows), no parent is named more than 2 times, and in every draw some parent is named exactly 2 times in some block; every parent has at least one child. `page_table`: the entries of each row are distinct; parent p's pool pages are rows p * 32 to p * 32 + 31 of kv_pool. `lengths`: the largest length is exactly 8.
All inputs are finite; a program needn't handle non-finite values. No bound on the sum of `lengths` on one device may be relied on, other than what follows from the above.
Results may differ from a plain program's by a relative error of at most 0.0048.
Values may be sent and summed in bfloat16 or wider, within the bound.
No kernel may reach another device: no remote copies, remote signals or barrier semaphores. Data moves between devices by JAX's collectives and lax.ppermute only.
A program may use at most 128 MiB of HBM per device.

v0:
```python
import jax
import jax.numpy as jnp
from jax import lax
from jax.sharding import PartitionSpec as P

MHEADS = 256
NSTATE = 256
GROUPS = 8
AHDIM = 128
CAP = 2


HIGH = lax.Precision.HIGHEST
NEGATIVE = -1e30
EPSILON = 1e-05


def causal_conv(history, incoming, kernel):
    joined = jnp.concatenate([history, incoming], axis=0).astype(jnp.float32)
    span_len = incoming.shape[0]
    summed = joined[0:span_len] * kernel[0]
    for offset in range(1, kernel.shape[0]):
        summed = summed + joined[offset : offset + span_len] * kernel[offset]
    return jax.nn.silu(summed)


def state_space(xconv, bmat, cmat, dt_raw, start, a_log, dt_bias, d_skip, head_share):
    span_len = xconv.shape[0]
    groups_here = bmat.shape[1]
    heads_here = dt_raw.shape[1]
    head_size = xconv.shape[1] // heads_here
    xsplit = xconv.reshape(span_len, groups_here, head_share, head_size)
    step_size = jax.nn.softplus(dt_raw.astype(jnp.float32) + dt_bias)
    decays = (step_size * -jnp.exp(a_log)).reshape(span_len, groups_here, head_share)
    running = jnp.cumsum(decays, axis=0)
    anchor = start.reshape(groups_here, head_share, head_size, -1)
    carried = (
        jnp.einsum("tgn,gpdn->tgpd", cmat, anchor, precision=HIGH) * jnp.exp(running)[:, :, :, None]
    )
    intersection = jnp.einsum("tgn,sgn->gts", cmat, bmat, precision=HIGH)
    causal = lax.broadcasted_iota(jnp.int32, (span_len, span_len), 0) >= lax.broadcasted_iota(
        jnp.int32, (span_len, span_len), 1
    )
    running_t = jnp.transpose(running, (1, 2, 0))
    spread = running_t[:, :, :, None] - running_t[:, :, None, :]
    kernel_ts = jnp.where(causal, jnp.exp(jnp.where(causal, spread, 0.0)), 0.0)
    steps_dt = jnp.transpose(step_size.reshape(span_len, groups_here, head_share), (1, 2, 0))
    weight = kernel_ts * steps_dt[:, :, None, :] * intersection[:, None]
    within = jnp.einsum("gpts,sgpd->tgpd", weight, xsplit, precision=HIGH)
    direct = d_skip.reshape(groups_here, head_share)[None, :, :, None] * xsplit
    return (carried + within + direct).reshape(span_len, heads_here * head_size)


def causal_mask(span_len):
    return lax.broadcasted_iota(jnp.int32, (span_len, span_len), 0) >= lax.broadcasted_iota(
        jnp.int32, (span_len, span_len), 1
    )


def full_attention(queries, prefix_keys, prefix_values, new_keys, new_values):
    span_len = queries.shape[0]
    kv_heads = prefix_keys.shape[-1] // AHDIM
    grouped = queries.reshape(span_len, kv_heads, -1, AHDIM)
    inverse_root = AHDIM ** (-0.5)
    keys_old = prefix_keys.reshape(-1, kv_heads, AHDIM)
    values_old = prefix_values.reshape(-1, kv_heads, AHDIM)
    keys_new = new_keys.reshape(-1, kv_heads, AHDIM)
    values_new = new_values.reshape(-1, kv_heads, AHDIM)
    prefix_scores = (
        jnp.einsum("tgqd,lgd->gqtl", grouped, keys_old, preferred_element_type=jnp.float32)
        * inverse_root
    )
    reply_scores = (
        jnp.einsum("tgqd,lgd->gqtl", grouped, keys_new, preferred_element_type=jnp.float32)
        * inverse_root
    )
    reply_scores = jnp.where(causal_mask(span_len), reply_scores, NEGATIVE)
    highest = jnp.maximum(jnp.max(prefix_scores, axis=-1), jnp.max(reply_scores, axis=-1))
    prefix_raw = jnp.exp(prefix_scores - highest[..., None])
    reply_raw = jnp.exp(reply_scores - highest[..., None])
    denominator = jnp.sum(prefix_raw, axis=-1) + jnp.sum(reply_raw, axis=-1)
    summed = jnp.einsum(
        "gqtl,lgd->tgqd",
        prefix_raw.astype(jnp.bfloat16),
        values_old,
        preferred_element_type=jnp.float32,
    )
    summed = summed + jnp.einsum(
        "gqtl,lgd->tgqd",
        reply_raw.astype(jnp.bfloat16),
        values_new,
        preferred_element_type=jnp.float32,
    )
    return (summed / jnp.transpose(denominator, (2, 0, 1))[..., None]).reshape(span_len, -1)


def pack_rows(placer, values, siblings):
    flat = values.reshape(values.shape[0], -1)
    packed = jnp.dot(placer, flat, preferred_element_type=jnp.float32).astype(values.dtype)
    return packed.reshape((siblings, -1) + values.shape[1:])


def unpack_rows(placer, values):
    flat = values.reshape(placer.shape[0], -1)
    result = jnp.dot(placer.T, flat, preferred_element_type=jnp.float32).astype(jnp.bfloat16)
    return result.reshape((placer.shape[1],) + values.shape[2:])


def local(
    reply_x,
    reply_bc,
    reply_dt,
    reply_gate,
    reply_query,
    reply_kv,
    lengths,
    fork_list,
    ssm_state,
    conv_x,
    conv_bc,
    kv_pool,
    page_table,
    kernel_x,
    kernel_bc,
    a_log,
    dt_bias,
    d_skip,
    norm_gain,
):
    branches = reply_x.shape[0]
    span_len = reply_x.shape[1]
    siblings = lax.axis_size("sibling")
    slot_count = siblings * CAP
    parent = fork_list[:, 0]
    row_ids = lax.broadcasted_iota(jnp.int32, (branches, branches), 0)
    col_ids = lax.broadcasted_iota(jnp.int32, (branches, branches), 1)
    earlier = jnp.logical_and(parent[:, None] == parent[None, :], col_ids < row_ids)
    rank_ids = jnp.sum(earlier.astype(jnp.int32), axis=1)
    slot_ids = parent * CAP + rank_ids
    placer = (
        lax.broadcasted_iota(jnp.int32, (slot_count, branches), 0) == slot_ids[None, :]
    ).astype(jnp.bfloat16)
    sent_x = pack_rows(placer, reply_x, siblings)
    sent_bc = pack_rows(placer, reply_bc, siblings)
    sent_dt = pack_rows(placer, reply_dt, siblings)
    got_x, got_bc, got_dt = (
        lax.all_to_all(sent_x, "sibling", split_axis=0, concat_axis=0, tiled=True),
        lax.all_to_all(sent_bc, "sibling", split_axis=0, concat_axis=0, tiled=True),
        lax.all_to_all(sent_dt, "sibling", split_axis=0, concat_axis=0, tiled=True),
    )
    slots_x = got_x.reshape((slot_count,) + reply_x.shape[1:])
    slots_bc = got_bc.reshape((slot_count,) + reply_bc.shape[1:])
    slots_dt = got_dt.reshape((slot_count,) + reply_dt.shape[1:])
    xconv = jax.vmap(causal_conv, in_axes=(None, 0, None))(conv_x[0], slots_x, kernel_x)
    bcconv = jax.vmap(causal_conv, in_axes=(None, 0, None))(conv_bc[0], slots_bc, kernel_bc)
    groups_here = reply_bc.shape[-1] // NSTATE
    bmat = bcconv[:, :, 0].reshape(slot_count, span_len, groups_here, NSTATE)
    cmat = bcconv[:, :, 1].reshape(slot_count, span_len, groups_here, NSTATE)
    start = ssm_state[0]

    def mix_one(x_one, b_one, c_one, dt_one):
        return state_space(
            x_one, b_one, c_one, dt_one, start, a_log, dt_bias, d_skip, MHEADS // GROUPS
        )

    mixed = jax.vmap(mix_one)(xconv, bmat, cmat, slots_dt)
    mixed = mixed.astype(jnp.bfloat16).reshape((siblings, CAP, span_len, -1))
    returned = lax.all_to_all(mixed, "sibling", split_axis=0, concat_axis=0, tiled=True)
    mixer = unpack_rows(placer, returned)
    gated = mixer.astype(jnp.float32) * jax.nn.silu(reply_gate.astype(jnp.float32))
    grouped = gated.reshape(branches, span_len, groups_here, -1)
    meansq = jnp.mean(grouped * grouped, axis=-1, keepdims=True)
    normed = (grouped * lax.rsqrt(meansq + EPSILON) * norm_gain.reshape(groups_here, -1)).reshape(
        branches, span_len, -1
    )
    valid = lax.broadcasted_iota(jnp.int32, (branches, span_len), 1) < lengths[:, None]
    mamba_out = jnp.where(valid[:, :, None], normed, 0.0).astype(jnp.bfloat16)
    ordered = kv_pool[page_table[0]]
    own_prefix = ordered.reshape(-1, 2, ordered.shape[-1])
    pair_shape = (branches // 2, 2)
    everyone = lax.all_gather(own_prefix, "sibling", axis=0, tiled=True)
    everyone = everyone.reshape((siblings, -1) + own_prefix.shape[1:])
    chosen = everyone[parent]

    def copy_pair(items):
        query_pair, prefix_pair, reply_pair = items
        return jax.vmap(full_attention)(
            query_pair,
            prefix_pair[:, :, 0],
            prefix_pair[:, :, 1],
            reply_pair[:, :, 0],
            reply_pair[:, :, 1],
        )

    attended = lax.map(
        copy_pair,
        (
            reply_query.reshape(pair_shape + reply_query.shape[1:]),
            chosen.reshape(pair_shape + chosen.shape[1:]),
            reply_kv.reshape(pair_shape + reply_kv.shape[1:]),
        ),
    )
    attended = attended.reshape(branches, span_len, -1)
    attn_out = jnp.where(valid[:, :, None], attended, 0.0).astype(jnp.bfloat16)
    return (mamba_out, attn_out)


def solution(mesh):
    return jax.shard_map(
        local,
        mesh=mesh,
        in_specs=(
            P(("replica", "sibling"), None, "tensor"),
            P(("replica", "sibling"), None, None, "tensor"),
            P(("replica", "sibling"), None, "tensor"),
            P(("replica", "sibling"), None, "tensor"),
            P(("replica", "sibling"), None, "tensor"),
            P(("replica", "sibling"), None, None, "tensor"),
            P(("replica", "sibling")),
            P(("replica", "sibling"), None),
            P(("replica", "sibling"), "tensor", None, None),
            P(("replica", "sibling"), None, "tensor"),
            P(("replica", "sibling"), None, None, "tensor"),
            P(("replica", "sibling"), None, None, "tensor"),
            P(("replica", "sibling"), None),
            P(None, "tensor"),
            P(None, None, "tensor"),
            P("tensor"),
            P("tensor"),
            P("tensor"),
            P("tensor"),
        ),
        out_specs=(
            P(("replica", "sibling"), None, "tensor"),
            P(("replica", "sibling"), None, "tensor"),
        ),
        check_vma=False,
    )
```

profile of v0, /device:TPU:96, one launch (start us, length us, event | category | flops | bytes accessed | tf_op | source)
XLA Modules:
  0.0 232.5 jit_solution(13689489216403794887)
XLA Ops:
  7.3 0.8 fusion.58
  8.1 0.7 copy-done
  8.8 2.7 %gather_fusion = bf16[16,128,2,128]{3,2,1,0:T(2,128)(2,1)S(1)} fusion(bf16[32,128,2,128]{3,2,1,0:T(2,128)(2,1)S(1)} %copy-done, s32[1024]{0:T(1024)S(1)} %pad_clamp_fusion.1), kind=kCustom, calls=%fused_computation | custom fusion | bytes 2097216 | tf_op jit(solution)/shard_map/gather | solution.py:178
  11.4 1.3 copy.96
  13.3 0.7 reshape.374
  14.0 7.0 %all-to-all-start.1 = ((bf16[16,2,256]{2,1,0:T(2,128)(2,1)}), bf16[16,2,256]{2,1,0:T(2,128)(2,1)S(1)}, u32[]{:S(2)}, u32[]{:S(2)}) async-start(bf16[16,2,256]{2,1,0:T(2,128)(2,1)} %reshape.374), calls=%async_computation.1 | async-start | bytes 32768 | tf_op jit(solution)/shard_map/all_to_all | solution.py:149
  21.1 1.3 copy.112
  23.2 0.9 reshape.331
  24.1 4.6 %all-to-all-done.1 = bf16[16,2,256]{2,1,0:T(2,128)(2,1)S(1)} async-done(((bf16[16,2,256]{2,1,0:T(2,128)(2,1)}), bf16[16,2,256]{2,1,0:T(2,128)(2,1)S(1)}, u32[]{:S(2)}, u32[]{:S(2)}) %all-to-all-start.1) | async-done | bytes 16416 | tf_op jit(solution)/shard_map/all_to_all | solution.py:149
  28.7 3.5 %all-to-all-start = ((bf16[16,2,8,2,256]{4,3,2,1,0:T(2,128)(2,1)}), bf16[16,2,8,2,256]{4,3,2,1,0:T(2,128)(2,1)S(1)}, u32[]{:S(2)}, u32[]{:S(2)}) async-start(bf16[16,2,8,2,256]{4,3,2,1,0:T(2,128)(2,1)} %reshape.331), calls=%async_computation | async-start | bytes 524288 | tf_op jit(solution)/shard_map/all_to_all | solution.py:148
  32.2 1.6 copy.113
  34.1 10.1 %all-to-all-done = bf16[16,2,8,2,256]{4,3,2,1,0:T(2,128)(2,1)S(1)} async-done(((bf16[16,2,8,2,256]{4,3,2,1,0:T(2,128)(2,1)}), bf16[16,2,8,2,256]{4,3,2,1,0:T(2,128)(2,1)S(1)}, u32[]{:S(2)}, u32[]{:S(2)}) %all-to-all-start) | async-done | bytes 262176 | tf_op jit(solution)/shard_map/all_to_all | solution.py:148
  44.2 3.8 %all-to-all-start.2 = ((bf16[16,2,8,2048]{3,2,1,0:T(8,128)(2,1)}), bf16[16,2,8,2048]{3,2,1,0:T(8,128)(2,1)S(1)}, u32[]{:S(2)}, u32[]{:S(2)}) async-start(bf16[16,2,8,2048]{3,2,1,0:T(8,128)(2,1)} %bitcast.89), calls=%async_computation.2 | async-start | bytes 2097152 | tf_op jit(solution)/shard_map/all_to_all | solution.py:147
  48.0 1.2 broadcast_multiply_fusion
  49.2 5.3 %reduce_window_sum.11 = f32[32,8,1,32]{1,3,0,2:T(8,128)S(1)} reduce-window(f32[32,8,1,32]{1,3,0,2:T(8,128)S(1)} %get-tuple-element.65, f32[]{:T(128)} %constant.27.clone.1), window={size=1x8x1x1 pad=0_0x7_0x0_0x0_0}, to_apply=%region_1.2 | reduce-window | flops 57344 | bytes 65540 | tf_op jit(solution)/shard_map/vmap(jit(cumsum))/reduce_window_sum | solution.py:35
  54.5 0.9 exponential_bitcast_fusion
  56.3 9.2 %all-to-all-done.2 = bf16[16,2,8,2048]{3,2,1,0:T(8,128)(2,1)S(1)} async-done(((bf16[16,2,8,2048]{3,2,1,0:T(8,128)(2,1)}), bf16[16,2,8,2048]{3,2,1,0:T(8,128)(2,1)S(1)}, u32[]{:S(2)}, u32[]{:S(2)}) %all-to-all-start.2) | async-done | bytes 1048608 | tf_op jit(solution)/shard_map/all_to_all | solution.py:147
  65.8 0.7 maximum_convert_fusion
  66.5 1.2 divide_multiply_fusion
  67.7 3.0 %reshape.340 = f32[32,8,32,64]{3,2,1,0:T(8,128)} reshape(f32[32,8,2048]{2,1,0:T(8,128)S(1)} %divide_multiply_fusion) | data formatting | bytes 4194304 | tf_op jit(solution)/shard_map/reshape.58
  70.7 3.0 %reshape.342 = f32[32,8,1,32,64]{4,3,1,0,2:T(8,128)} reshape(f32[32,8,2048]{2,1,0:T(8,128)S(1)} %divide_multiply_fusion) | data formatting | bytes 4194304 | tf_op jit(solution)/shard_map/vmap()/reshape | solution.py:32
  73.8 13.1 %fusion.22 = f32[32,32,64,8]{2,3,1,0:T(8,128)S(1)} fusion(f32[32,8,32,64]{3,2,1,0:T(8,128)} %reshape.340, f32[32,8,8]{2,1,0:T(8,128)S(1)} %fusion.48, f32[32,32,8]{2,1,0:T(8,128)} %bitcast.215, f32[32,32,8]{2,1,0:T(8,128)S(1)} %bitcast.211, pred[8,8]{1,0:T(8,128)(4,1)S(1)} %iota_compare_fusion.8), kind=kOutput, calls=%fused_computation.45 | convolution fusion | flops 50659328 | bytes 4268096 | tf_op jit(solution)/shard_map/vmap(gpts,sgpd->tgpd)/dot_general | solution.py:49
  86.9 8.5 %fusion.21 = bf16[32,8,1,32,64]{4,1,3,0,2:T(8,128)(2,1)S(1)} fusion(f32[32,32,64,8]{2,3,1,0:T(8,128)S(1)} %fusion.22, f32[32,8,1,32,64]{4,3,1,0,2:T(8,128)S(1)} %copy-done.2, f32[1,32,64,256]{3,2,1,0:T(8,128)S(1)} %copy-done.3, f32[32]{0:T(128)S(1)} %copy-done.15, f32[32,8,32]{1,2,0:T(8,128)S(1)} %copy-done.4, f32[32,8,2,256]{3,1,0,2:T(8,128)S(1)} %divide_multiply_fusion.1), kind=kOutput, calls=%fused_computation.42 | convolution fusion | flops 1613234176 | bytes 12321280 | tf_op jit(solution)/shard_map/vmap(tgn,gpdn->tgpd)/dot_general | solution.py:38
  95.9 2.4 %convert_element_type.76 = bf16[16,2,8,2048]{3,2,1,0:T(8,128)(2,1)} reshape(bf16[32,8,1,32,64]{4,3,1,0,2:T(8,128)(2,1)S(1)} %copy.95) | data formatting | bytes 2097152 | tf_op jit(solution)/shard_map/convert_element_type | solution.py:167
  98.4 3.8 %all-to-all-start.3 = ((bf16[16,2,8,2048]{3,2,1,0:T(8,128)(2,1)}), bf16[16,2,8,2048]{3,2,1,0:T(8,128)(2,1)S(1)}, u32[]{:S(2)}, u32[]{:S(2)}) async-start(bf16[16,2,8,2048]{3,2,1,0:T(8,128)(2,1)} %convert_element_type.76), calls=%async_computation.3 | async-start | bytes 2097152 | tf_op jit(solution)/shard_map/all_to_all | solution.py:168
  102.3 28.3 %all-to-all-done.3 = bf16[16,2,8,2048]{3,2,1,0:T(8,128)(2,1)S(1)} async-done(((bf16[16,2,8,2048]{3,2,1,0:T(8,128)(2,1)}), bf16[16,2,8,2048]{3,2,1,0:T(8,128)(2,1)S(1)}, u32[]{:S(2)}, u32[]{:S(2)}) %all-to-all-start.3) | async-done | bytes 1048608 | tf_op jit(solution)/shard_map/all_to_all | solution.py:168
  130.6 0.6 copy.114
  131.5 0.6 copy.115
  132.6 1.0 select_convert_fusion
  133.6 22.0 %all-gather.2.cloned.1.call-done = bf16[32768,2,128]{2,0,1:T(8,128)(2,1)} async-done(((bf16[2048,2,128]{2,0,1:T(8,128)(2,1)}), bf16[32768,2,128]{2,0,1:T(8,128)(2,1)}) %all-gather.2.cloned.1.call-update) | async-done | bytes 16777232 | tf_op jit(solution)/shard_map/all_gather | solution.py:181
  155.6 13.7 %copy.97 = bf16[16,2048,2,128]{3,1,2,0:T(8,128)(2,1)} copy(bf16[16,2048,2,128]{3,1,0,2:T(8,128)(2,1)} %bitcast.204) | data formatting | bytes 33554432 | tf_op jit(solution)/shard_map/reshape | solution.py:182
  169.3 13.0 %gather_fusion.1 = bf16[16,2048,2,128]{3,1,2,0:T(8,128)(2,1)} fusion(bf16[16,2048,2,128]{3,1,2,0:T(8,128)(2,1)} %copy.97, s32[1024]{0:T(1024)S(1)} %pad_clamp_fusion), kind=kCustom, calls=%fused_computation.1 | custom fusion | bytes 33554496 | tf_op jit(solution)/shard_map/gather | solution.py:183
  182.4 41.5 %while.10 = (s32[]{:T(128)}, bf16[8,2,8,1024]{3,2,1,0:T(8,128)(2,1)S(1)}, bf16[8,2,2048,2,128]{4,2,3,1,0:T(8,128)(2,1)}, bf16[8,2,8,1024]{3,2,1,0:T(8,128)(2,1)}, bf16[8,2,8,2,128]{4,3,2,1,0:T(2,128)(2,1)}, /*index=5*/s32[]{:T(128)}) while((s32[]{:T(128)}, bf16[8,2,8,1024]{3,2,1,0:T(8,128)(2,1)S(1)}, bf16[8,2,2048,2,128]{4,2,3,1,0:T(8,128)(2,1)}, ...), condition=%wide.region_8.9_spmd, body=%wide.region_3.8_spmd.sunk | while | flops 136091456 | bytes 9869969 | solution.py:195
  182.4 1.7 copy_bitcast_fusion.3
  184.1 0.8 dynamic-slice_bitcast_fusion.2
  184.9 0.6 fusion.79
  185.5 0.7 constant_dynamic-slice_fusion.6
  187.6 1.7 copy_bitcast_fusion.3
  189.3 0.8 dynamic-slice_bitcast_fusion.2
  190.6 0.7 constant_dynamic-slice_fusion.6
  192.8 1.7 copy_bitcast_fusion.3
  194.5 0.8 dynamic-slice_bitcast_fusion.2
  195.3 0.6 fusion.79
  195.8 0.7 constant_dynamic-slice_fusion.6
  198.0 1.7 copy_bitcast_fusion.3
  199.7 0.8 dynamic-slice_bitcast_fusion.2
  201.0 0.7 constant_dynamic-slice_fusion.6
  203.2 1.7 copy_bitcast_fusion.3
  204.9 0.8 dynamic-slice_bitcast_fusion.2
  205.7 0.6 fusion.79
  206.2 0.7 constant_dynamic-slice_fusion.6
  208.4 1.7 copy_bitcast_fusion.3
  210.1 0.8 dynamic-slice_bitcast_fusion.2
  210.9 0.6 fusion.79
  211.4 0.7 constant_dynamic-slice_fusion.6
  213.6 1.7 copy_bitcast_fusion.3
  215.3 0.8 dynamic-slice_bitcast_fusion.2
  216.1 0.6 fusion.79
  216.6 0.7 constant_dynamic-slice_fusion.6
  218.8 1.7 copy_bitcast_fusion.3
  220.5 0.8 dynamic-slice_bitcast_fusion.2
  221.8 0.7 constant_dynamic-slice_fusion.6
  224.0 0.8 fusion.47
  224.8 0.9 copy-done.1
  (158 shorter events, 16.7 us)
Async XLA Ops:
  7.2 1.6 copy-start
  7.2 5.6 %copy-start.7 = (bf16[16,8,32]{2,1,0:T(8,128)(2,1)S(1)}, bf16[16,8,32]{2,1,0:T(8,128)(2,1)}, u32[]{:S(2)}) copy-start(bf16[16,8,32]{2,1,0:T(8,128)(2,1)} %param.23) | copy-start | bytes 24580
  7.2 5.7 %copy-start.17 = (s32[16,1]{0,1:T(1,128)S(1)}, s32[16,1]{0,1:T(1,128)}, u32[]{:S(2)}) copy-start(s32[16,1]{0,1:T(1,128)} %param.28) | copy-start | bytes 196
  7.2 15.2 %copy-start.6 = (bf16[16,8,2,256]{3,2,1,0:T(2,128)(2,1)S(1)}, bf16[16,8,2,256]{3,2,1,0:T(2,128)(2,1)}, u32[]{:S(2)}) copy-start(bf16[16,8,2,256]{3,2,1,0:T(2,128)(2,1)} %param.22) | copy-start | bytes 393220
  7.2 148.4 %all-gather.2.cloned.1.call-start = ((), (), s32[]{:S(2)}) async-start(), calls=%async_computation.4 | async-start | bytes 17825792 | tf_op jit(solution)/shard_map/all_gather | solution.py:181
  8.8 14.4 %copy-start.8 = (f32[4,2048]{1,0:T(4,128)S(1)}, f32[4,2048]{1,0:T(4,128)}, u32[]{:S(2)}) copy-start(f32[4,2048]{1,0:T(4,128)} %param.34) | copy-start | bytes 98308
  8.8 14.4 %copy-start.16 = (f32[32]{0:T(128)S(1)}, f32[32]{0:T(128)}, u32[]{:S(2)}) copy-start(f32[32]{0:T(128)} %param.36) | copy-start | bytes 388
  12.8 21.0 %copy-start.12 = (bf16[1,3,2,256]{3,2,1,0:T(2,128)(2,1)S(1)}, bf16[1,3,2,256]{3,2,1,0:T(2,128)(2,1)}, u32[]{:S(2)}) copy-start(bf16[1,3,2,256]{3,2,1,0:T(2,128)(2,1)} %param.31) | copy-start | bytes 9220
  12.8 21.0 %copy-start.11 = (f32[4,2,256]{2,1,0:T(2,128)S(1)}, f32[4,2,256]{2,1,0:T(2,128)}, u32[]{:S(2)}) copy-start(f32[4,2,256]{2,1,0:T(2,128)} %param.35) | copy-start | bytes 24580
  14.0 14.6 %all-to-all-start.1 = ((bf16[16,2,256]{2,1,0:T(2,128)(2,1)}), bf16[16,2,256]{2,1,0:T(2,128)(2,1)S(1)}, u32[]{:S(2)}, u32[]{:S(2)}) async-start(bf16[16,2,256]{2,1,0:T(2,128)(2,1)} %reshape.374), calls=%async_computation.1 | async-start | bytes 32768 | tf_op jit(solution)/shard_map/all_to_all | solution.py:149
  22.4 25.6 %copy-start.13 = (f32[32]{0:T(128)S(1)}, f32[32]{0:T(128)}, u32[]{:S(2)}) copy-start(f32[32]{0:T(128)} %param.37) | copy-start | bytes 388
  28.7 15.5 %all-to-all-start = ((bf16[16,2,8,2,256]{4,3,2,1,0:T(2,128)(2,1)}), bf16[16,2,8,2,256]{4,3,2,1,0:T(2,128)(2,1)S(1)}, u32[]{:S(2)}, u32[]{:S(2)}) async-start(bf16[16,2,8,2,256]{4,3,2,1,0:T(2,128)(2,1)} %reshape.331), calls=%async_computation | async-start | bytes 524288 | tf_op jit(solution)/shard_map/all_to_all | solution.py:148
  44.2 21.4 %all-to-all-start.2 = ((bf16[16,2,8,2048]{3,2,1,0:T(8,128)(2,1)}), bf16[16,2,8,2048]{3,2,1,0:T(8,128)(2,1)S(1)}, u32[]{:S(2)}, u32[]{:S(2)}) async-start(bf16[16,2,8,2048]{3,2,1,0:T(8,128)(2,1)} %bitcast.89), calls=%async_computation.2 | async-start | bytes 2097152 | tf_op jit(solution)/shard_map/all_to_all | solution.py:147
  48.0 17.5 %copy-start.9 = (bf16[1,3,2048]{2,1,0:T(4,128)(2,1)S(1)}, bf16[1,3,2048]{2,1,0:T(4,128)(2,1)}, u32[]{:S(2)}) copy-start(bf16[1,3,2048]{2,1,0:T(4,128)(2,1)} %param.30) | copy-start | bytes 36868
  73.8 13.1 %copy-start.2 = (f32[32,8,1,32,64]{4,3,1,0,2:T(8,128)S(1)}, f32[32,8,1,32,64]{4,3,1,0,2:T(8,128)}, u32[]{:S(2)}) copy-start(f32[32,8,1,32,64]{4,3,1,0,2:T(8,128)} %reshape.342) | copy-start | bytes 6291460
  73.8 13.1 %copy-start.3 = (f32[1,32,64,256]{3,2,1,0:T(8,128)S(1)}, f32[1,32,64,256]{3,2,1,0:T(8,128)}, u32[]{:S(2)}) copy-start(f32[1,32,64,256]{3,2,1,0:T(8,128)} %param.29) | copy-start | bytes 6291460
  73.8 13.1 %copy-start.4 = (f32[32,8,32]{1,2,0:T(8,128)S(1)}, f32[32,8,32]{1,2,0:T(8,128)}, u32[]{:S(2)}) copy-start(f32[32,8,32]{1,2,0:T(8,128)} %exponential_bitcast_fusion) | copy-start | bytes 98308
  73.8 13.1 %copy-start.15 = (f32[32]{0:T(128)S(1)}, f32[32]{0:T(128)}, u32[]{:S(2)}) copy-start(f32[32]{0:T(128)} %param.38) | copy-start | bytes 388
  95.4 6.8 %copy-start.14 = (s32[16]{0:T(128)S(1)}, s32[16]{0:T(128)}, u32[]{:S(2)}) copy-start(s32[16]{0:T(128)} %param.27) | copy-start | bytes 196
  98.4 33.8 %copy-start.5 = (bf16[16,8,2048]{2,1,0:T(8,128)(2,1)S(1)}, bf16[16,8,2048]{2,1,0:T(8,128)(2,1)}, u32[]{:S(2)}) copy-start(bf16[16,8,2048]{2,1,0:T(8,128)(2,1)} %param.24) | copy-start | bytes 1572868
  98.4 32.2 %all-to-all-start.3 = ((bf16[16,2,8,2048]{3,2,1,0:T(8,128)(2,1)}), bf16[16,2,8,2048]{3,2,1,0:T(8,128)(2,1)S(1)}, u32[]{:S(2)}, u32[]{:S(2)}) async-start(bf16[16,2,8,2048]{3,2,1,0:T(8,128)(2,1)} %convert_element_type.76), calls=%async_computation.3 | async-start | bytes 2097152 | tf_op jit(solution)/shard_map/all_to_all | solution.py:168
  131.2 1.5 copy-start.10
  224.0 1.7 copy-start.1
Sparse Core Ops, SparseCore 0:
  12.9 142.6 all-gather.1
where the time goes:
time: 236 us; the launch traced here: 232 us
  local copies, waits for them, and re-layouts  75.9 us (32%)
  waiting for transfers between devices  74.2 us (31%)
  matrix products  34.1 us (14%)
  starting transfers between devices  18.2 us (8%)
  other arithmetic  15.1 us (6%)
  between operations  14.4 us (6%)
    all_to_all x1, waiting for transfers between devices, local(): lax.all_to_all(mixed, 'sibling', split_axis=0, concat_axis=0, tiled=True)  28.3 us
    all_gather x1, waiting for transfers between devices, local(): everyone = lax.all_gather(own_prefix, 'sibling', axis=0, tiled=True)  22 us
    squeeze x8, local copies, waits for them, and re-layouts, local(): lax.map(copy_pair, (reply_query.reshape(pair_shape + reply_query.shape[1:...  13.8 us
    reshape x1, local copies, waits for them, and re-layouts, local(): everyone = everyone.reshape((siblings, -1) + own_prefix.shape[1:])  13.7 us
    dot_general x1, matrix products, state_space(): within = jnp.einsum('gpts,sgpd->tgpd', weight, xsplit, precision=HIGH)  13.1 us
    gather x1, local copies, waits for them, and re-layouts, local(): chosen = everyone[parent]  13 us
    all_to_all x1, waiting for transfers between devices, local(): lax.all_to_all(sent_bc, 'sibling', split_axis=0, concat_axis=0, tiled=True)  10.1 us
    all_to_all x1, waiting for transfers between devices, local(): lax.all_to_all(sent_x, 'sibling', split_axis=0, concat_axis=0, tiled=True)  9.19 us
  transfers between devices with their start and end apart: 5, of which 5 were waited for; matrix products, arithmetic and copies ran while one was open for 22% of the time, Pallas kernels for 0%

commit v1 on v0

v1 whole, which is shorter than its diff:
```python
import math

import jax
import jax.numpy as jnp
from jax import lax
from jax.experimental import pallas as pl
from jax.experimental.pallas import tpu as pltpu
from jax.sharding import PartitionSpec as P

AHDIM = 128
CAP = 2
NEGATIVE = -1e30
EPSILON = 1e-05
F32 = jnp.float32
BF16 = jnp.bfloat16

Q_ROWS = 64
KV_ROWS = 16
C_ROWS = 16
SLOT_ROWS = Q_ROWS + KV_ROWS + C_ROWS
HIST_AT = CAP * SLOT_ROWS
HIST_ROWS = 80
SEND_ROWS = HIST_AT + HIST_ROWS
LIMIT = 50 * 1024 * 1024


def whole(memory_space=pltpu.VMEM):
    return pl.BlockSpec(memory_space=memory_space)


def silu(v):
    return v / (1.0 + jnp.exp(-v))


def fold(x, rows):
    return jnp.concatenate([x[:, i : i + 128] for i in range(0, x.shape[1], 128)], axis=0)


def unfold(x, rows):
    return jnp.concatenate([x[i : i + rows] for i in range(0, x.shape[0], rows)], axis=1)


def place_of(fork, count, child):
    parent = fork[child, 0]
    rank = jnp.minimum(count[parent], CAP - 1)
    count[parent] = count[parent] + 1
    return parent, rank


def clear(count):
    for parent in range(count.shape[0]):
        count[parent] = 0


def spread_bc(bc, rows_bc):
    for i, part in enumerate(rows_bc):
        part[...] = bc[:, :, 128 * i : 128 * i + 128].astype(F32).reshape(part.shape)


def pack_kernel(fork, query, news, bc, conv_x, conv_bc, send, count, *rows_bc):
    children = query.shape[0]
    clear(count)
    send[:, 0:HIST_AT, :] = jnp.zeros((send.shape[0], HIST_AT, 128), BF16)
    spread_bc(bc, rows_bc)
    own_x = conv_x[0].astype(F32)
    pairs = [conv_bc[0, row].astype(F32) for row in range(3)]
    own_b = jnp.concatenate([pair[0:1] for pair in pairs], axis=0)
    own_c = jnp.concatenate([pair[1:2] for pair in pairs], axis=0)
    own = jnp.concatenate([own_x, own_b, own_c], axis=1)
    own = jnp.concatenate([own, jnp.zeros((1, own.shape[1]), F32)], axis=0)
    history = fold(own, 4).astype(BF16)
    for parent in range(send.shape[0]):
        send[parent, HIST_AT:SEND_ROWS, :] = history
    for child in range(children):
        parent, rank = place_of(fork, count, child)
        rows_q = fold(query[child].astype(F32), 8).astype(BF16)
        rows_c = [part[pl.ds(16 * child + 1, 8, stride=2), :] for part in rows_bc]
        rows_c = jnp.concatenate(rows_c, axis=0).astype(BF16)
        block = jnp.concatenate([rows_q, news[child], rows_c], axis=0)
        send[parent, pl.ds(pl.multiple_of(rank * SLOT_ROWS, 32), SLOT_ROWS), :] = block


def prefix_kernel(table, page, state, keys, values, state_hi, state_lo, rows):
    rows[...] = page[0].astype(F32)
    keys[...] = rows[pl.ds(0, 128, stride=2), :].astype(BF16)
    values[:, 0:128] = rows[pl.ds(1, 128, stride=2), :].astype(BF16)
    values[:, 128:256] = jnp.ones((128, 128), BF16)
    high = state[...].astype(BF16)
    state_hi[...] = high
    state_lo[...] = (state[...] - high.astype(F32)).astype(BF16)


def transposed_dot(a, b):
    return lax.dot_general(a, b, (((1,), (1,)), ((), ())), preferred_element_type=F32)


def parent_kernel(got, keys, values, state_hi, state_lo, conv_bc, kernel_bc, back, rows):
    senders = got.shape[0]
    raw = []
    for slot in range(CAP):
        at = slot * SLOT_ROWS + Q_ROWS + KV_ROWS
        part = got[:, at : at + C_ROWS, :].astype(F32)
        raw.append(jnp.concatenate([part[:, 0:8], part[:, 8:16]], axis=2))
    raw = jnp.concatenate(raw, axis=1).reshape(senders * CAP * 8, 256)
    old = [conv_bc[0, row].astype(F32)[1:2] for row in range(3)]
    token = lax.broadcasted_iota(jnp.int32, (senders * CAP, 8, 256), 1)
    taps = [kernel_bc[tap][1:2] for tap in range(4)]
    total = raw * taps[3]
    for lag in range(1, 4):
        early = jnp.concatenate(old[3 - lag :] + [jnp.zeros((8 - lag, 256), F32)], axis=0)
        moved = pltpu.roll(raw, lag, 0).reshape(senders * CAP, 8, 256)
        joined = jnp.where(token < lag, early[None], moved).reshape(raw.shape)
        total = total + joined * taps[3 - lag]
    cmat = silu(total)
    c_hi = cmat.astype(BF16)
    c_lo = (cmat - c_hi.astype(F32)).astype(BF16)
    channels = state_hi.shape[0]
    for at in range(0, channels, 256):
        high = state_hi[at : at + 256, :]
        read = transposed_dot(c_hi, high) + transposed_dot(c_lo, high)
        read = read + transposed_dot(c_hi, state_lo[at : at + 256, :])
        back[:, :, :, at : at + 256] = read.astype(BF16).reshape(senders, CAP, 8, 256)

    factor = AHDIM**-0.5 * math.log2(math.e)
    row_ids = lax.broadcasted_iota(jnp.int32, (256, 32), 0)
    col_ids = lax.broadcasted_iota(jnp.int32, (256, 32), 1)
    seen = jnp.logical_and(row_ids // 64 == col_ids // 8, row_ids % 8 >= col_ids % 8)

    def block(step, carry):
        sender = 2 * step
        places = [(sender + i, slot * SLOT_ROWS) for i in range(2) for slot in range(CAP)]
        queries = jnp.concatenate([got[s, at : at + Q_ROWS, :] for s, at in places], axis=0)
        at_kv = [(s, at + Q_ROWS) for s, at in places]
        rows[...] = jnp.concatenate(
            [got[s, at : at + KV_ROWS, :].astype(F32) for s, at in at_kv], axis=0
        )
        new_keys = rows[pl.ds(0, 32, stride=2), :].astype(BF16)
        new_values = rows[pl.ds(1, 32, stride=2), :].astype(BF16)
        new_values = jnp.concatenate([new_values, jnp.ones((32, 128), BF16)], axis=1)
        scores = transposed_dot(queries, keys[...])
        reply = jnp.where(seen, transposed_dot(queries, new_keys), NEGATIVE)
        highest = jnp.maximum(
            jnp.max(scores, axis=1, keepdims=True), jnp.max(reply, axis=1, keepdims=True)
        )
        weights = jnp.exp2((scores - highest) * factor).astype(BF16)
        reply_weights = jnp.exp2((reply - highest) * factor).astype(BF16)
        summed = jnp.dot(weights, values[...], preferred_element_type=F32)
        summed = summed + jnp.dot(reply_weights, new_values, preferred_element_type=F32)
        attended = summed[:, 0:128] / summed[:, 128:256]
        for i in range(2 * CAP):
            one = unfold(attended[64 * i : 64 * i + 64], 8)
            back[sender + i // CAP, i % CAP, :, channels:] = one.astype(BF16)
        return carry

    lax.fori_loop(0, senders // 2, block, 0)


def child_kernel(
    fork, got, reply_x, bc, dt, gate, kernel_x, kernel_bc, params,
    within, fade, gates, history, weights, *rows_bc,
):
    children = reply_x.shape[0]
    count = children * 8
    for child in range(children):
        own = got[fork[child, 0], HIST_AT:SEND_ROWS, :].astype(F32)
        history[8 * child : 8 * child + 4, :] = unfold(own, 4)
        history[8 * child + 4 : 8 * child + 8, :] = jnp.zeros((4, history.shape[1]), F32)

    def convolve(raw, old, taps):
        token = lax.broadcasted_iota(jnp.int32, raw.shape, 0) % 8
        total = raw * taps[3]
        for lag in range(1, 4):
            early = old if lag == 3 else pltpu.roll(old, count - (3 - lag), 0)
            joined = jnp.where(token < lag, early, pltpu.roll(raw, lag, 0))
            total = total + joined * taps[3 - lag]
        return silu(total)

    spread_bc(bc, rows_bc)
    channels = reply_x.shape[2]
    state = bc.shape[2]
    mats = []
    for part in range(2):
        raw = [half[pl.ds(part, count, stride=2), :] for half in rows_bc]
        raw = jnp.concatenate(raw, axis=1)
        at = channels + part * state
        taps = [kernel_bc[tap][part : part + 1] for tap in range(4)]
        mats.append(convolve(raw, history[:, at : at + state], taps))
    bmat = mats[0].reshape(children, 8, state)
    cmat = mats[1].reshape(children, 8, state)

    heads = dt.shape[2]
    spread = lax.broadcasted_iota(jnp.int32, (heads, 128), 1) % heads
    spread = (spread == lax.broadcasted_iota(jnp.int32, (heads, 128), 0)).astype(BF16)
    raw_dt = jnp.dot(
        dt[...].astype(F32).reshape(count, heads).astype(BF16), spread, preferred_element_type=F32
    )
    shifted = raw_dt + params[1:2]
    step_size = jnp.maximum(shifted, 0.0) + jnp.log1p(jnp.exp(-jnp.abs(shifted)))
    running = step_size * -jnp.exp(params[0:1])
    token = lax.broadcasted_iota(jnp.int32, (count, 128), 0) % 8
    for hop in (1, 2, 4):
        running = running + jnp.where(token >= hop, pltpu.roll(running, hop, 0), 0.0)
    lane = lax.broadcasted_iota(jnp.int32, (count, 128), 1) // heads

    def put(at, value):
        high = value.astype(BF16).astype(F32)
        rest = value - high
        middle = rest.astype(BF16).astype(F32)
        low = rest - middle
        parts = jnp.where(lane == 0, high, jnp.where(lane == 1, middle, jnp.where(lane == 2, low, 0.0)))
        weights[at * count : (at + 1) * count, :] = parts.astype(BF16)

    token3 = lax.broadcasted_iota(jnp.int32, (children, 8, 128), 1)
    running3 = running.reshape(children, 8, 128)
    step3 = step_size.reshape(children, 8, 128)
    skip = params[2:3][None]
    for source in range(8):
        overlap = jnp.sum(cmat * bmat[:, source : source + 1, :], axis=2, keepdims=True)
        later = token3 >= source
        span = jnp.where(later, running3 - running3[:, source : source + 1, :], 0.0)
        value = jnp.where(later, jnp.exp(span) * step3[:, source : source + 1, :] * overlap, 0.0)
        value = value + jnp.where(token3 == source, skip, 0.0)
        put(source, value.reshape(count, 128))
    put(8, jnp.exp(running))

    per = 256
    for at in range(0, channels, per):
        raw = reply_x[:, :, at : at + per].astype(F32).reshape(count, per)
        taps = [kernel_x[tap : tap + 1, at : at + per] for tap in range(4)]
        xconv = convolve(raw, history[:, at : at + per], taps).reshape(children, 8, per)
        head = at // 64 + lax.broadcasted_iota(jnp.int32, (128, per), 1) // 64
        source_head = lax.broadcasted_iota(jnp.int32, (128, per), 0) % heads
        spread_x = (head == source_head).astype(BF16)
        wide = jnp.dot(weights[...], spread_x, preferred_element_type=F32)
        total = None
        for source in range(8):
            weight = wide[source * count : (source + 1) * count].reshape(children, 8, per)
            term = weight * xconv[:, source : source + 1, :]
            total = term if total is None else total + term
        within[:, :, at : at + per] = total
        fade[:, :, at : at + per] = wide[8 * count :].reshape(children, 8, per)
        gates[:, :, at : at + per] = silu(gate[:, :, at : at + per].astype(F32))


def finish_kernel(fork, lengths, got, within, fade, gates, gain, mamba, attn, count):
    clear(count)
    channels = within.shape[2]
    for child in range(within.shape[0]):
        parent, rank = place_of(fork, count, child)
        length = lengths[child]
        read = got[parent, rank].astype(F32)
        mixer = fade[child] * read[:, 0:channels] + within[child]
        gated = mixer.astype(BF16).astype(F32) * gates[child]
        meansq = jnp.mean(gated * gated, axis=1, keepdims=True)
        normed = gated * lax.rsqrt(meansq + EPSILON) * gain[...]
        token = lax.broadcasted_iota(jnp.int32, (8, 1), 0)
        mamba[child] = jnp.where(token < length, normed, 0.0).astype(BF16)
        attn[child] = jnp.where(token < length, read[:, channels:], 0.0).astype(BF16)


def params_of(flops, bytes_accessed, transcendentals=0):
    return dict(
        compiler_params=pltpu.CompilerParams(vmem_limit_bytes=LIMIT),
        cost_estimate=pl.CostEstimate(
            flops=flops, bytes_accessed=bytes_accessed, transcendentals=transcendentals
        ),
    )


def local(
    reply_x,
    reply_bc,
    reply_dt,
    reply_gate,
    reply_query,
    reply_kv,
    lengths,
    fork_list,
    ssm_state,
    conv_x,
    conv_bc,
    kv_pool,
    page_table,
    kernel_x,
    kernel_bc,
    a_log,
    dt_bias,
    d_skip,
    norm_gain,
):
    children, tokens, channels = reply_x.shape
    siblings = lax.axis_size("sibling")
    state = ssm_state.shape[3]
    widths = reply_query.shape[2]
    heads = a_log.shape[0]
    news = reply_kv.reshape(children, 2 * tokens, AHDIM)
    bc = reply_bc.reshape(children, 2 * tokens, state)
    pool = kv_pool.reshape(kv_pool.shape[0], 256, AHDIM)
    flat_state = ssm_state.reshape(channels, state)
    params = jnp.tile(jnp.stack([a_log, dt_bias, d_skip]), (1, 128 // heads))
    gain = norm_gain.reshape(1, channels)

    halves = [pltpu.VMEM((children * 2 * tokens, 128), F32)] * (state // 128)

    send = pl.pallas_call(
        pack_kernel,
        out_shape=jax.ShapeDtypeStruct((siblings, SEND_ROWS, 128), BF16),
        in_specs=[whole(pltpu.SMEM)] + [whole()] * 5,
        out_specs=whole(),
        scratch_shapes=[pltpu.SMEM((siblings,), jnp.int32)] + halves,
        **params_of(1_000_000, 2_000_000),
    )(fork_list, reply_query, news, bc, conv_x, conv_bc)
    got = lax.all_to_all(send, "sibling", split_axis=0, concat_axis=0, tiled=True)

    pages = page_table.shape[1]
    share = channels // pages
    keys, values, state_hi, state_lo = pl.pallas_call(
        prefix_kernel,
        out_shape=(
            jax.ShapeDtypeStruct((pages * 128, AHDIM), BF16),
            jax.ShapeDtypeStruct((pages * 128, 2 * AHDIM), BF16),
            jax.ShapeDtypeStruct((channels, state), BF16),
            jax.ShapeDtypeStruct((channels, state), BF16),
        ),
        grid_spec=pltpu.PrefetchScalarGridSpec(
            num_scalar_prefetch=1,
            grid=(pages,),
            in_specs=[
                pl.BlockSpec((1, 256, AHDIM), lambda i, table: (table[0, i], 0, 0)),
                pl.BlockSpec((share, state), lambda i, table: (i, 0)),
            ],
            out_specs=[
                pl.BlockSpec((128, AHDIM), lambda i, table: (i, 0)),
                pl.BlockSpec((128, 2 * AHDIM), lambda i, table: (i, 0)),
                pl.BlockSpec((share, state), lambda i, table: (i, 0)),
                pl.BlockSpec((share, state), lambda i, table: (i, 0)),
            ],
            scratch_shapes=[pltpu.VMEM((256, AHDIM), F32)],
        ),
        **params_of(4_000_000, 8_000_000),
    )(page_table, pool, flat_state)

    back = pl.pallas_call(
        parent_kernel,
        out_shape=jax.ShapeDtypeStruct((siblings, CAP, tokens, channels + widths), BF16),
        in_specs=[whole()] * 7,
        out_specs=whole(),
        scratch_shapes=[pltpu.VMEM((64, AHDIM), F32)],
        **params_of(6_000_000_000, 8_000_000, 4_000_000),
    )(got, keys, values, state_hi, state_lo, conv_bc, kernel_bc)
    returned = lax.all_to_all(back, "sibling", split_axis=0, concat_axis=0, tiled=True)

    wide = jax.ShapeDtypeStruct((children, tokens, channels), F32)
    within, fade, gates = pl.pallas_call(
        child_kernel,
        out_shape=(wide, wide, wide),
        in_specs=[whole(pltpu.SMEM)] + [whole()] * 8,
        out_specs=(whole(), whole(), whole()),
        scratch_shapes=[
            pltpu.VMEM((children * tokens, channels + 2 * state), F32),
            pltpu.VMEM((9 * children * tokens, 128), BF16),
        ]
        + halves,
        **params_of(600_000_000, 8_000_000, 1_000_000),
    )(fork_list, got, reply_x, bc, reply_dt, reply_gate, kernel_x, kernel_bc, params)

    return pl.pallas_call(
        finish_kernel,
        out_shape=(
            jax.ShapeDtypeStruct((children, tokens, channels), BF16),
            jax.ShapeDtypeStruct((children, tokens, widths), BF16),
        ),
        in_specs=[whole(pltpu.SMEM), whole(pltpu.SMEM)] + [whole()] * 5,
        out_specs=(whole(), whole()),
        scratch_shapes=[pltpu.SMEM((siblings,), jnp.int32)],
        **params_of(10_000_000, 6_000_000),
    )(fork_list, lengths, returned, within, fade, gates, gain)


def solution(mesh):
    return jax.shard_map(
        local,
        mesh=mesh,
        in_specs=(
            P(("replica", "sibling"), None, "tensor"),
            P(("replica", "sibling"), None, None, "tensor"),
            P(("replica", "sibling"), None, "tensor"),
            P(("replica", "sibling"), None, "tensor"),
            P(("replica", "sibling"), None, "tensor"),
            P(("replica", "sibling"), None, None, "tensor"),
            P(("replica", "sibling")),
            P(("replica", "sibling"), None),
            P(("replica", "sibling"), "tensor", None, None),
            P(("replica", "sibling"), None, "tensor"),
            P(("replica", "sibling"), None, None, "tensor"),
            P(("replica", "sibling"), None, None, "tensor"),
            P(("replica", "sibling"), None),
            P(None, "tensor"),
            P(None, None, "tensor"),
            P("tensor"),
            P("tensor"),
            P("tensor"),
            P("tensor"),
        ),
        out_specs=(
            P(("replica", "sibling"), None, "tensor"),
            P(("replica", "sibling"), None, "tensor"),
        ),
        check_vma=False,
    )
```

time: 236 us -> 81.3 us (0.34); the launches traced: 232 us -> 80.6 us
  local copies, waits for them, and re-layouts: 75.9 us -> 8.08 us
  waiting for transfers between devices: 74.2 us -> 24.7 us
  Pallas kernels: 0 us -> 35.3 us
  matrix products: 34.1 us -> 0 us
  other arithmetic: 15.1 us -> 0.01 us
  between operations: 14.4 us -> 0.8 us
  starting transfers between devices: 18.2 us -> 11.6 us
    pallas_call x0 -> x5, Pallas kernels: none -> 35.3 us  [the longest x1 15.7 us: local(): pl.pallas_call(parent_kernel, out_shape=jax.ShapeDtypeStruct((siblings, C...]
    dot_general x39 -> x0, matrix products: 34.1 us -> none  [the longest x1 13.1 us: state_space(): within = jnp.einsum('gpts,sgpd->tgpd', weight, xsplit, precision=HIGH)]
    all_to_all x4 -> x2, waiting for transfers between devices: 52.2 us -> 24.7 us  [the longest x1 15.8 us: local(): lax.all_to_all(back, 'sibling', split_axis=0, concat_axis=0, tiled=True)]
    all_gather x1 -> x0, waiting for transfers between devices: 22 us -> none  [local(): everyone = lax.all_gather(own_prefix, 'sibling', axis=0, tiled=True)]
    gather x3 -> x0, local copies, waits for them, and re-layouts: 17 us -> none  [the longest x1 13 us: local(): chosen = everyone[parent]]
    reshape x6 -> x1, local copies, waits for them, and re-layouts: 17.9 us -> 0.96 us  [local(): bc = reply_bc.reshape(children, 2 * tokens, state)]
    squeeze x9 -> x0, local copies, waits for them, and re-layouts: 13.8 us -> none  [the longest x8 13.8 us: local(): lax.map(copy_pair, (reply_query.reshape(pair_shape + reply_query.shape[1:...]
    all_to_all x4 -> x2, starting transfers between devices: 18.2 us -> 11.6 us  [the longest x1 7.08 us: local(): lax.all_to_all(send, 'sibling', split_axis=0, concat_axis=0, tiled=True)]
  transfers between devices with their start and end apart: 5 -> 2, of which waited for: 5 -> 2; matrix products, arithmetic and copies ran while one was open for 22% -> 0% of each run, Pallas kernels for 0% -> 19%
where the time goes in v1:
time: 81.3 us; the launch traced here: 80.6 us
  Pallas kernels  35.3 us (43%)
  waiting for transfers between devices  24.7 us (30%)
  starting transfers between devices  11.6 us (14%)
  local copies, waits for them, and re-layouts  8.08 us (10%)
    all_to_all x1, waiting for transfers between devices, local(): lax.all_to_all(back, 'sibling', split_axis=0, concat_axis=0, tiled=True)  15.8 us
    pallas_call x1, Pallas kernels, local(): pl.pallas_call(parent_kernel, out_shape=jax.ShapeDtypeStruct((siblings, C...  15.7 us
    all_to_all x1, waiting for transfers between devices, local(): lax.all_to_all(send, 'sibling', split_axis=0, concat_axis=0, tiled=True)  8.89 us
    pallas_call x1, Pallas kernels, local(): pl.pallas_call(prefix_kernel, out_shape=(jax.ShapeDtypeStruct((pages * 12...  8.76 us
    all_to_all x1, starting transfers between devices, local(): lax.all_to_all(send, 'sibling', split_axis=0, concat_axis=0, tiled=True)  7.08 us
    unnamed x39, local copies, waits for them, and re-layouts  7.04 us
    pallas_call x1, Pallas kernels, local(): pl.pallas_call(child_kernel, out_shape=(wide, wide, wide), in_specs=[whol...  6.21 us
    all_to_all x1, starting transfers between devices, local(): lax.all_to_all(back, 'sibling', split_axis=0, concat_axis=0, tiled=True)  4.55 us
  transfers between devices with their start and end apart: 2, of which 2 were waited for; matrix products, arithmetic and copies ran while one was open for 0% of the time, Pallas kernels for 19%

profile of v1, /device:TPU:96, one launch (start us, length us, event | category | flops | bytes accessed | tf_op | source)
XLA Modules:
  0.0 80.6 jit_solution(162843092871269653)
XLA Ops:
  0.6 0.7 copy.23.fork
  1.4 1.0 %reshape.24.bc = bf16[16,16,256]{2,1,0:T(8,128)(2,1)S(1)} reshape(bf16[16,8,2,256]{3,2,1,0:T(2,128)(2,1)} %param.20) | data formatting | bytes 262144 | tf_op jit(solution)/shard_map/reshape | solution.py:297
  2.3 0.0 copy-start.3
  2.3 0.9 %copy-done.3 = bf16[16,8,1024]{2,1,0:T(8,128)(2,1)S(1)} copy-done((bf16[16,8,1024]{2,1,0:T(8,128)(2,1)S(1)}, bf16[16,8,1024]{2,1,0:T(8,128)(2,1)}, u32[]{:S(2)}) %copy-start.3) | copy-done | bytes 262168
  3.3 0.0 copy-start.4
  3.3 0.8 %copy-done.4 = bf16[16,8,2,128]{3,2,1,0:T(2,128)(2,1)S(1)} copy-done((bf16[16,8,2,128]{3,2,1,0:T(2,128)(2,1)S(1)}, bf16[16,8,2,128]{3,2,1,0:T(2,128)(2,1)}, u32[]{:S(2)}) %copy-start.4) | copy-done | bytes 65560
  4.1 0.0 copy-start.7
  4.1 0.7 copy-done.7
  4.8 0.0 copy-start.10
  4.8 0.7 copy-done.10
  5.5 0.0 copy-start.12
  5.5 1.9 %shard_map.194 = bf16[16,272,128]{2,1,0:T(8,128)(2,1)} custom-call(s32[16,1]{1,0:T(8,128)S(1)} %copy.23.fork, bf16[16,8,1024]{2,1,0:T(8,128)(2,1)S(1)} %copy-done.3, bf16[16,16,128]{2,1,0:T(8,128)(2,1)S(1)} %bitcast.7, bf16[16,16,256]{2,1,0:T(8,128)(2,1)S(1)} %reshape.24.bc, bf16[1,3,2048]{2,1,0:T(4,128)(2,1)S(1)} %copy-done.7, ...), custom_call_target="tpu_custom_call" | custom-call | flops 1000000 | bytes 2000000 | tf_op jit(solution)/shard_map/pallas_call | solution.py:305
  7.4 7.1 %all-to-all-start = ((bf16[16,272,128]{2,1,0:T(8,128)(2,1)}), bf16[16,272,128]{2,1,0:T(8,128)(2,1)}, u32[]{:S(2)}, u32[]{:S(2)}) async-start(bf16[16,272,128]{2,1,0:T(8,128)(2,1)} %shard_map.194), calls=%async_computation | async-start | bytes 2228224 | tf_op jit(solution)/shard_map/all_to_all | solution.py:313
  14.5 0.0 copy-done.12
  14.5 0.0 copy-start.8
  14.5 0.0 copy-start.11
  14.5 8.8 %shard_map.195 = (bf16[2048,128]{1,0:T(8,128)(2,1)S(1)}, bf16[2048,256]{1,0:T(8,128)(2,1)S(1)}, bf16[2048,256]{1,0:T(8,128)(2,1)S(1)}, bf16[2048,256]{1,0:T(8,128)(2,1)S(1)}) custom-call(s32[1,16]{1,0:T(1,128)S(1)} %copy-done.12, bf16[32,256,128]{2,1,0:T(8,128)(2,1)} %bitcast.9, f32[2048,256]{1,0:T(8,128)} %bitcast.10), custom_call_target="tpu_custom_call" | custom-call | flops 4000000 | bytes 8000000 | tf_op jit(solution)/shard_map/pallas_call | solution.py:317
  23.3 0.0 copy-start.14
  23.3 0.8 copy-done.14
  24.1 8.9 %all-to-all-done.got = bf16[16,272,128]{2,1,0:T(8,128)(2,1)} async-done(((bf16[16,272,128]{2,1,0:T(8,128)(2,1)}), bf16[16,272,128]{2,1,0:T(8,128)(2,1)}, u32[]{:S(2)}, u32[]{:S(2)}) %all-to-all-start) | async-done | bytes 1114144 | tf_op jit(solution)/shard_map/all_to_all | solution.py:313
  33.0 0.0 copy-done.8
  33.0 0.0 copy-done.11
  33.0 0.0 copy-start.15
  33.0 1.0 %copy-done.15 = bf16[2048,128]{1,0:T(8,128)(2,1)S(1)} copy-done((bf16[2048,128]{1,0:T(8,128)(2,1)S(1)}, bf16[2048,128]{1,0:T(8,128)(2,1)}, u32[]{:S(2)}) %copy-start.15) | copy-done | bytes 524312
  34.0 15.7 %shard_map.196 = bf16[16,2,8,3072]{3,2,1,0:T(8,128)(2,1)} custom-call(bf16[16,272,128]{2,1,0:T(8,128)(2,1)} %all-to-all-done.got, bf16[2048,128]{1,0:T(8,128)(2,1)S(1)} %copy-done.15, bf16[2048,256]{1,0:T(8,128)(2,1)S(1)} %get-tuple-element.10.values, bf16[2048,256]{1,0:T(8,128)(2,1)S(1)} %get-tuple-element.11.state_hi, ...), custom_call_target="tpu_custom_call" | custom-call | flops 6000000000 | bytes 8000000 | tf_op jit(solution)/shard_map/pallas_call | solution.py:343
  49.8 0.0 copy-start.16
  49.8 0.0 copy-start.17
  49.8 0.0 copy-start.18
  49.8 0.0 copy-start.1
  49.8 0.0 copy-start.2
  49.8 0.0 copy-start.5
  49.8 0.0 copy-start.6
  49.8 4.6 %all-to-all-start.1 = ((bf16[16,2,8,3072]{3,2,1,0:T(8,128)(2,1)}), bf16[16,2,8,3072]{3,2,1,0:T(8,128)(2,1)}, u32[]{:S(2)}, u32[]{:S(2)}) async-start(bf16[16,2,8,3072]{3,2,1,0:T(8,128)(2,1)} %shard_map.196), calls=%async_computation.1 | async-start | bytes 3145728 | tf_op jit(solution)/shard_map/all_to_all | solution.py:351
  54.4 0.0 copy-start.9
  54.4 0.0 copy-start.13
  54.4 0.0 copy-done.16
  54.4 0.0 copy-done.17
  54.4 0.0 copy-done.18
  54.4 0.1 tile.10.params
  54.5 0.0 copy-done.1
  54.5 0.0 copy-done.2
  54.5 0.0 copy-done.5
  54.5 0.0 copy-done.6
  54.5 6.2 %shard_map.197 = (f32[16,8,2048]{2,1,0:T(8,128)S(1)}, f32[16,8,2048]{2,1,0:T(8,128)S(1)}, f32[16,8,2048]{2,1,0:T(8,128)}) custom-call(s32[16,1]{1,0:T(8,128)S(1)} %copy.23.fork, bf16[16,272,128]{2,1,0:T(8,128)(2,1)} %all-to-all-done.got, bf16[16,8,2048]{2,1,0:T(8,128)(2,1)S(1)} %copy-done.1, bf16[16,16,256]{2,1,0:T(8,128)(2,1)S(1)} %reshape.24.bc, ...), custom_call_target="tpu_custom_call" | custom-call | flops 600000000 | bytes 8000000 | tf_op jit(solution)/shard_map/pallas_call | solution.py:354
  60.7 15.8 %all-to-all-done.1.got = bf16[16,2,8,3072]{3,2,1,0:T(8,128)(2,1)} async-done(((bf16[16,2,8,3072]{3,2,1,0:T(8,128)(2,1)}), bf16[16,2,8,3072]{3,2,1,0:T(8,128)(2,1)}, u32[]{:S(2)}, u32[]{:S(2)}) %all-to-all-start.1) | async-done | bytes 1572896 | tf_op jit(solution)/shard_map/all_to_all | solution.py:351
  76.6 0.0 copy-done.9
  76.6 0.0 copy-done.13
  76.6 0.0 copy-start
  76.6 1.2 %copy-done = f32[16,8,2048]{2,1,0:T(8,128)S(1)} copy-done((f32[16,8,2048]{2,1,0:T(8,128)S(1)}, f32[16,8,2048]{2,1,0:T(8,128)}, u32[]{:S(2)}) %copy-start) | copy-done | bytes 1048600
  77.8 2.8 %shard_map.198 = (bf16[16,8,2048]{2,1,0:T(8,128)(2,1)}, bf16[16,8,1024]{2,1,0:T(8,128)(2,1)}) custom-call(s32[16,1]{1,0:T(8,128)S(1)} %copy.23.fork, s32[16]{0:T(128)S(1)} %copy-done.13, bf16[16,2,8,3072]{3,2,1,0:T(8,128)(2,1)} %all-to-all-done.1.got, f32[16,8,2048]{2,1,0:T(8,128)S(1)} %get-tuple-element.13.within, ...), custom_call_target="tpu_custom_call" | custom-call | flops 10000000 | bytes 6000000 | tf_op jit(solution)/shard_map/pallas_call | solution.py:367
  (2 shorter events, 0.0 us)
Async XLA Ops:
  2.3 1.0 %copy-start.3 = (bf16[16,8,1024]{2,1,0:T(8,128)(2,1)S(1)}, bf16[16,8,1024]{2,1,0:T(8,128)(2,1)}, u32[]{:S(2)}) copy-start(bf16[16,8,1024]{2,1,0:T(8,128)(2,1)} %query.1) | copy-start | bytes 786436
  3.3 0.8 %copy-start.4 = (bf16[16,8,2,128]{3,2,1,0:T(2,128)(2,1)S(1)}, bf16[16,8,2,128]{3,2,1,0:T(2,128)(2,1)}, u32[]{:S(2)}) copy-start(bf16[16,8,2,128]{3,2,1,0:T(2,128)(2,1)} %param.24) | copy-start | bytes 196612
  4.1 0.7 copy-start.7
  4.8 0.7 copy-start.10
  5.5 9.0 %copy-start.12 = (s32[1,16]{1,0:T(1,128)S(1)}, s32[1,16]{1,0:T(1,128)}, u32[]{:S(2)}) copy-start(s32[1,16]{1,0:T(1,128)} %table.1) | copy-start | bytes 196
  7.4 25.6 %all-to-all-start = ((bf16[16,272,128]{2,1,0:T(8,128)(2,1)}), bf16[16,272,128]{2,1,0:T(8,128)(2,1)}, u32[]{:S(2)}, u32[]{:S(2)}) async-start(bf16[16,272,128]{2,1,0:T(8,128)(2,1)} %shard_map.194), calls=%async_computation | async-start | bytes 2228224 | tf_op jit(solution)/shard_map/all_to_all | solution.py:313
  14.5 18.5 %copy-start.8 = (f32[4,2,256]{2,1,0:T(2,128)S(1)}, f32[4,2,256]{2,1,0:T(2,128)}, u32[]{:S(2)}) copy-start(f32[4,2,256]{2,1,0:T(2,128)} %kernel_bc.3) | copy-start | bytes 24580
  14.5 18.5 %copy-start.11 = (bf16[1,3,2,256]{3,2,1,0:T(2,128)(2,1)S(1)}, bf16[1,3,2,256]{3,2,1,0:T(2,128)(2,1)}, u32[]{:S(2)}) copy-start(bf16[1,3,2,256]{3,2,1,0:T(2,128)(2,1)} %conv_bc.3) | copy-start | bytes 9220
  23.3 0.8 copy-start.14
  33.0 1.0 %copy-start.15 = (bf16[2048,128]{1,0:T(8,128)(2,1)S(1)}, bf16[2048,128]{1,0:T(8,128)(2,1)}, u32[]{:S(2)}) copy-start(bf16[2048,128]{1,0:T(8,128)(2,1)} %copy-done.14) | copy-start | bytes 1572868
  49.8 4.6 %copy-start.16 = (f32[32]{0:T(128)S(1)}, f32[32]{0:T(128)}, u32[]{:S(2)}) copy-start(f32[32]{0:T(128)} %param.36) | copy-start | bytes 388
  49.8 4.6 %copy-start.17 = (f32[32]{0:T(128)S(1)}, f32[32]{0:T(128)}, u32[]{:S(2)}) copy-start(f32[32]{0:T(128)} %param.35) | copy-start | bytes 388
  49.8 4.6 %copy-start.18 = (f32[32]{0:T(128)S(1)}, f32[32]{0:T(128)}, u32[]{:S(2)}) copy-start(f32[32]{0:T(128)} %param.34) | copy-start | bytes 388
  49.8 4.8 %copy-start.1 = (bf16[16,8,2048]{2,1,0:T(8,128)(2,1)S(1)}, bf16[16,8,2048]{2,1,0:T(8,128)(2,1)}, u32[]{:S(2)}) copy-start(bf16[16,8,2048]{2,1,0:T(8,128)(2,1)} %reply_x.1) | copy-start | bytes 1572868
  49.8 4.8 %copy-start.2 = (bf16[16,8,2048]{2,1,0:T(8,128)(2,1)S(1)}, bf16[16,8,2048]{2,1,0:T(8,128)(2,1)}, u32[]{:S(2)}) copy-start(bf16[16,8,2048]{2,1,0:T(8,128)(2,1)} %gate.1) | copy-start | bytes 1572868
  49.8 4.8 %copy-start.5 = (bf16[16,8,32]{2,1,0:T(8,128)(2,1)S(1)}, bf16[16,8,32]{2,1,0:T(8,128)(2,1)}, u32[]{:S(2)}) copy-start(bf16[16,8,32]{2,1,0:T(8,128)(2,1)} %dt.1) | copy-start | bytes 24580
  49.8 4.7 %copy-start.6 = (f32[4,2048]{1,0:T(4,128)S(1)}, f32[4,2048]{1,0:T(4,128)}, u32[]{:S(2)}) copy-start(f32[4,2048]{1,0:T(4,128)} %kernel_x.1) | copy-start | bytes 98308
  49.8 26.8 %all-to-all-start.1 = ((bf16[16,2,8,3072]{3,2,1,0:T(8,128)(2,1)}), bf16[16,2,8,3072]{3,2,1,0:T(8,128)(2,1)}, u32[]{:S(2)}, u32[]{:S(2)}) async-start(bf16[16,2,8,3072]{3,2,1,0:T(8,128)(2,1)} %shard_map.196), calls=%async_computation.1 | async-start | bytes 3145728 | tf_op jit(solution)/shard_map/all_to_all | solution.py:351
  54.4 22.2 %copy-start.9 = (f32[2048]{0:T(1024)S(1)}, f32[2048]{0:T(1024)}, u32[]{:S(2)}) copy-start(f32[2048]{0:T(1024)} %param.37) | copy-start | bytes 24580
  54.4 22.2 %copy-start.13 = (s32[16]{0:T(128)S(1)}, s32[16]{0:T(128)}, u32[]{:S(2)}) copy-start(s32[16]{0:T(128)} %lengths.1) | copy-start | bytes 196
  76.6 1.2 %copy-start = (f32[16,8,2048]{2,1,0:T(8,128)S(1)}, f32[16,8,2048]{2,1,0:T(8,128)}, u32[]{:S(2)}) copy-start(f32[16,8,2048]{2,1,0:T(8,128)} %get-tuple-element.15.gates) | copy-start | bytes 3145732

commit v2 on v1

v2 whole, which is shorter than its diff:
```python
import math

import jax
import jax.numpy as jnp
from jax import lax
from jax.experimental import pallas as pl
from jax.experimental.pallas import tpu as pltpu
from jax.sharding import PartitionSpec as P

AHDIM = 128
CAP = 2
PREFIX_ARRAYS = 32
HISTORY_ROOM = 1024
NEGATIVE = -1e30
EPSILON = 1e-05
F32 = jnp.float32
BF16 = jnp.bfloat16

Q_ROWS = 64
KV_ROWS = 16
C_ROWS = 16
SLOT_ROWS = Q_ROWS + KV_ROWS + C_ROWS
HIST_AT = CAP * SLOT_ROWS
HIST_ROWS = 64
SEND_ROWS = HIST_AT + HIST_ROWS


def whole(memory_space=pltpu.VMEM):
    return pl.BlockSpec(memory_space=memory_space)


def silu(v):
    return v / (1.0 + jnp.exp(-v))


def fold(x, rows):
    return jnp.concatenate([x[:, i : i + 128] for i in range(0, x.shape[1], 128)], axis=0)


def unfold(x, rows):
    return jnp.concatenate([x[i : i + rows] for i in range(0, x.shape[0], rows)], axis=1)


def place_of(fork, count, child):
    parent = fork[child]
    rank = jnp.minimum(count[parent], CAP - 1)
    count[parent] = count[parent] + 1
    return parent, rank


def clear(count):
    for parent in range(count.shape[0]):
        count[parent] = 0


def bc_rows(rows_bc, part, at, count):
    start = 4 * at + part
    return [rows_bc[pl.ds(start + 2 * half, count, stride=4), :] for half in range(2)]


def pack_kernel(*refs):
    sources, (send, count), held, (sems, rows_bc) = refs[:6], refs[6:8], refs[8:14], refs[14:]
    copies = [
        pltpu.make_async_copy(source, kept, sems.at[i])
        for i, (source, kept) in enumerate(zip(sources, held))
    ]
    for copy in copies:
        copy.start()
    bc, conv_x, conv_bc, fork, query, news = held
    children = query.shape[0]
    clear(count)
    send[:, 0:HIST_AT, :] = jnp.zeros((send.shape[0], HIST_AT, 128), BF16)
    for copy in copies[:3]:
        copy.wait()
    rows_bc[...] = bc[...].astype(F32).reshape(rows_bc.shape)
    own_x = conv_x[0].astype(F32)
    pairs = [conv_bc[0, row].astype(F32) for row in range(3)]
    own_b = jnp.concatenate([pair[0:1] for pair in pairs], axis=0)
    own_c = jnp.concatenate([pair[1:2] for pair in pairs], axis=0)
    own = jnp.concatenate([own_x, own_b, own_c], axis=1)
    history = jnp.concatenate([fold(own, 3), jnp.zeros((4, 128), F32)], axis=0).astype(BF16)
    for parent in range(send.shape[0]):
        send[parent, HIST_AT:SEND_ROWS, :] = history
    for copy in copies[3:]:
        copy.wait()
    for child in range(children):
        parent, rank = place_of(fork, count, child)
        rows_q = fold(query[child].astype(F32), 8).astype(BF16)
        rows_c = jnp.concatenate(bc_rows(rows_bc, 1, 8 * child, 8), axis=0).astype(BF16)
        block = jnp.concatenate([rows_q, news[child], rows_c], axis=0)
        send[parent, pl.ds(pl.multiple_of(rank * SLOT_ROWS, 32), SLOT_ROWS), :] = block


def prefix_kernel(table, page, prefix, rows):
    rows[...] = page[0].astype(F32)
    for part in range(2):
        prefix[part] = rows[pl.ds(part, 128, stride=2), :].astype(BF16)


def transposed_dot(a, b):
    return lax.dot_general(a, b, (((1,), (1,)), ((), ())), preferred_element_type=F32)


def parent_kernel(
    got, conv_bc, kernel_bc, prefix_hbm, state_hbm, back, history,
    keys, values, state, read_rows, attn_rows, rows, sems, sems_out,
):
    senders = got.shape[0]
    pairs = [
        (prefix_hbm.at[0], keys),
        (prefix_hbm.at[1], values.at[:, pl.ds(0, 128)]),
        (state_hbm, state),
    ]
    loads = [pltpu.make_async_copy(*pair, sems.at[i]) for i, pair in enumerate(pairs)]
    for load in loads:
        load.start()
    old_rows = got.at[:, pl.ds(HIST_AT, HIST_ROWS), :]
    outs = [pltpu.make_async_copy(old_rows, history.at[pl.ds(0, senders)], sems_out.at[0])]
    outs[0].start()
    values[:, 128:256] = jnp.ones((values.shape[0], 128), BF16)
    raw = []
    for slot in range(CAP):
        at = slot * SLOT_ROWS + Q_ROWS + KV_ROWS
        part = got[:, at : at + C_ROWS, :].astype(F32)
        raw.append(jnp.concatenate([part[:, 0:8], part[:, 8:16]], axis=2))
    raw = jnp.concatenate(raw, axis=1).reshape(senders * CAP * 8, 256)
    old = [conv_bc[0, row].astype(F32)[1:2] for row in range(3)]
    token = lax.broadcasted_iota(jnp.int32, (senders * CAP, 8, 256), 1)
    taps = [kernel_bc[tap][1:2] for tap in range(4)]
    total = raw * taps[3]
    for lag in range(1, 4):
        early = jnp.concatenate(old[3 - lag :] + [jnp.zeros((8 - lag, 256), F32)], axis=0)
        moved = pltpu.roll(raw, lag, 0).reshape(senders * CAP, 8, 256)
        joined = jnp.where(token < lag, early[None], moved).reshape(raw.shape)
        total = total + joined * taps[3 - lag]
    cmat = silu(total)
    c_hi = cmat.astype(BF16)
    c_lo = (cmat - c_hi.astype(F32)).astype(BF16)
    channels = state.shape[0]

    factor = AHDIM**-0.5 * math.log2(math.e)
    row_ids = lax.broadcasted_iota(jnp.int32, (256, 32), 0)
    col_ids = lax.broadcasted_iota(jnp.int32, (256, 32), 1)
    seen = jnp.logical_and(row_ids // 64 == col_ids // 8, row_ids % 8 >= col_ids % 8)
    for load in loads[0:2]:
        load.wait()

    def attend(at):
        sender = 2 * at
        places = [(sender + i, slot * SLOT_ROWS) for i in range(2) for slot in range(CAP)]
        queries = jnp.concatenate([got[s, at : at + Q_ROWS, :] for s, at in places], axis=0)
        kv_places = [(s, at + Q_ROWS) for s, at in places]
        fresh = [got[s, at : at + KV_ROWS, :].astype(F32) for s, at in kv_places]
        mine = rows.at[at]
        mine[...] = jnp.concatenate(fresh, axis=0)
        new_keys = mine[pl.ds(0, 32, stride=2), :].astype(BF16)
        new_values = mine[pl.ds(1, 32, stride=2), :].astype(BF16)
        new_values = jnp.concatenate([new_values, jnp.ones((32, 128), BF16)], axis=1)
        scores = transposed_dot(queries, keys[...])
        reply = jnp.where(seen, transposed_dot(queries, new_keys), NEGATIVE)
        highest = jnp.maximum(
            jnp.max(scores, axis=1, keepdims=True), jnp.max(reply, axis=1, keepdims=True)
        )
        weights = jnp.exp2((scores - highest) * factor).astype(BF16)
        reply_weights = jnp.exp2((reply - highest) * factor).astype(BF16)
        summed = jnp.dot(weights, values[...], preferred_element_type=F32)
        summed = summed + jnp.dot(reply_weights, new_values, preferred_element_type=F32)
        attended = summed[:, 0:128] / summed[:, 128:256]
        for i in range(2 * CAP):
            one = unfold(attended[64 * i : 64 * i + 64], 8)
            attn_rows[at, i // CAP, i % CAP] = one.astype(BF16)

    def send_attended(at):
        target = back.at[pl.ds(2 * at, 2), :, :, pl.ds(channels, attn_rows.shape[4])]
        outs.append(pltpu.make_async_copy(attn_rows.at[at], target, sems_out.at[2 + at]))
        outs[-1].start()

    blocks = attn_rows.shape[0]
    for at in range(blocks // 2):
        attend(at)
    loads[2].wait()
    for at in range(0, channels, 256):
        part = state[at : at + 256, :]
        high = part.astype(BF16)
        low = (part - high.astype(F32)).astype(BF16)
        read = transposed_dot(c_hi, high) + transposed_dot(c_lo, high) + transposed_dot(c_hi, low)
        read_rows[:, :, :, at : at + 256] = read.astype(BF16).reshape(senders, CAP, 8, 256)
    outs.append(
        pltpu.make_async_copy(read_rows, back.at[:, :, :, pl.ds(0, channels)], sems_out.at[1])
    )
    outs[-1].start()
    for at in range(blocks // 2):
        send_attended(at)
    for at in range(blocks // 2, blocks):
        attend(at)
    for at in range(blocks // 2, blocks):
        send_attended(at)
    for copy in outs:
        copy.wait()


def to_channels(at, count, heads):
    head = at // 64 + lax.broadcasted_iota(jnp.int32, (128, count), 1) // 64
    source_head = lax.broadcasted_iota(jnp.int32, (128, count), 0) % heads
    return (head == source_head).astype(BF16)


def child_kernel(
    fork, old_rows_hbm, reply_x, bc, dt, kernel_x, kernel_bc, params,
    within, fade, old_rows, history, weights, rows_bc, sem,
):
    load = pltpu.make_async_copy(old_rows_hbm.at[pl.ds(0, old_rows.shape[0])], old_rows, sem)
    load.start()
    load.wait()
    children = reply_x.shape[0]
    count = children * 8
    for child in range(children):
        own = unfold(old_rows[fork[child]].astype(F32)[0:60], 3)
        history[8 * child : 8 * child + 8, :] = jnp.concatenate(
            [own, jnp.zeros((5, own.shape[1]), F32)], axis=0
        )

    def convolve(raw, old, taps):
        token = lax.broadcasted_iota(jnp.int32, raw.shape, 0) % 8
        total = raw * taps[3]
        for lag in range(1, 4):
            early = old if lag == 3 else pltpu.roll(old, count - (3 - lag), 0)
            joined = jnp.where(token < lag, early, pltpu.roll(raw, lag, 0))
            total = total + joined * taps[3 - lag]
        return silu(total)

    rows_bc[...] = bc[...].astype(F32).reshape(rows_bc.shape)
    channels = reply_x.shape[2]
    state = 256
    mats = []
    for part in range(2):
        raw = jnp.concatenate(bc_rows(rows_bc, part, 0, count), axis=1)
        at = channels + part * state
        taps = [kernel_bc[tap][part : part + 1] for tap in range(4)]
        mats.append(convolve(raw, history[:, at : at + state], taps))
    bmat = mats[0].reshape(children, 8, state)
    cmat = mats[1].reshape(children, 8, state)

    heads = dt.shape[2]
    spread = lax.broadcasted_iota(jnp.int32, (heads, 128), 1) % heads
    spread = (spread == lax.broadcasted_iota(jnp.int32, (heads, 128), 0)).astype(BF16)
    raw_dt = jnp.dot(
        dt[...].astype(F32).reshape(count, heads).astype(BF16), spread, preferred_element_type=F32
    )
    shifted = raw_dt + params[1:2]
    step_size = jnp.maximum(shifted, 0.0) + jnp.log1p(jnp.exp(-jnp.abs(shifted)))
    running = step_size * -jnp.exp(params[0:1])
    token = lax.broadcasted_iota(jnp.int32, (count, 128), 0) % 8
    for hop in (1, 2, 4):
        running = running + jnp.where(token >= hop, pltpu.roll(running, hop, 0), 0.0)
    lane = lax.broadcasted_iota(jnp.int32, (count, 128), 1) // heads

    def split(value):
        high = value.astype(BF16).astype(F32)
        rest = value - high
        middle = rest.astype(BF16).astype(F32)
        low = rest - middle
        parts = jnp.where(lane == 0, high, jnp.where(lane == 1, middle, jnp.where(lane == 2, low, 0.0)))
        return parts.astype(BF16)

    token3 = lax.broadcasted_iota(jnp.int32, (children, 8, 128), 1)
    running3 = running.reshape(children, 8, 128)
    step3 = step_size.reshape(children, 8, 128)
    skip = params[2:3][None]
    for source in range(8):
        overlap = jnp.sum(cmat * bmat[:, source : source + 1, :], axis=2, keepdims=True)
        later = token3 >= source
        span = jnp.where(later, running3 - running3[:, source : source + 1, :], 0.0)
        value = jnp.where(later, jnp.exp(span) * step3[:, source : source + 1, :] * overlap, 0.0)
        value = value + jnp.where(token3 == source, skip, 0.0)
        weights[source * count : (source + 1) * count, :] = split(value.reshape(count, 128))
    fade[...] = split(jnp.exp(running))

    per = 256
    for at in range(0, channels, per):
        raw = reply_x[:, :, at : at + per].astype(F32).reshape(count, per)
        taps = [kernel_x[tap : tap + 1, at : at + per] for tap in range(4)]
        xconv = convolve(raw, history[:, at : at + per], taps).reshape(children, 8, per)
        wide = jnp.dot(weights[...], to_channels(at, per, heads), preferred_element_type=F32)
        total = None
        for source in range(8):
            weight = wide[source * count : (source + 1) * count].reshape(children, 8, per)
            term = weight * xconv[:, source : source + 1, :]
            total = term if total is None else total + term
        within[:, :, at : at + per] = total


def finish_kernel(
    fork_any, lengths_any, got, gain, fade, within, gate, mamba, attn,
    count, fork, lengths, wide, mamba_rows, attn_rows, sems, sems_out,
):
    loads = [
        pltpu.make_async_copy(fork_any, fork, sems.at[0]),
        pltpu.make_async_copy(lengths_any, lengths, sems.at[1]),
    ]
    for load in loads:
        load.start()
    clear(count)
    children, _, channels = within.shape
    heads = channels // 64
    for at in range(0, channels, 256):
        some = jnp.dot(fade[...], to_channels(at, 256, heads), preferred_element_type=F32)
        wide[:, :, at : at + 256] = some.reshape(children, 8, 256)
    for load in loads:
        load.wait()
    per = 4
    token = lax.broadcasted_iota(jnp.int32, (8, 1), 0)
    places = [place_of(fork, count, child) for child in range(children)]
    outs = []
    for at in range(children // per):
        for child in range(per * at, per * at + per):
            parent, rank = places[child]
            read = got[parent, rank].astype(F32)
            mixer = wide[child] * read[:, 0:channels] + within[child]
            gated = mixer.astype(BF16).astype(F32) * silu(gate[child].astype(F32))
            meansq = jnp.mean(gated * gated, axis=1, keepdims=True)
            normed = gated * lax.rsqrt(meansq + EPSILON) * gain[...]
            valid = token < lengths[child]
            mamba_rows[child] = jnp.where(valid, normed, 0.0).astype(BF16)
            attn_rows[child] = jnp.where(valid, read[:, channels:], 0.0).astype(BF16)
        part = pl.ds(per * at, per)
        for i, (rows, out) in enumerate(((mamba_rows, mamba), (attn_rows, attn))):
            outs.append(pltpu.make_async_copy(rows.at[part], out.at[part], sems_out.at[i, at]))
            outs[-1].start()
    for copy in outs:
        copy.wait()


def params_of(mebibytes, flops, bytes_accessed, transcendentals=0):
    return dict(
        compiler_params=pltpu.CompilerParams(vmem_limit_bytes=mebibytes * 1024 * 1024),
        cost_estimate=pl.CostEstimate(
            flops=flops, bytes_accessed=bytes_accessed, transcendentals=transcendentals
        ),
    )


def local(
    reply_x,
    reply_bc,
    reply_dt,
    reply_gate,
    reply_query,
    reply_kv,
    lengths,
    fork_list,
    ssm_state,
    conv_x,
    conv_bc,
    kv_pool,
    page_table,
    kernel_x,
    kernel_bc,
    a_log,
    dt_bias,
    d_skip,
    norm_gain,
):
    children, tokens, channels = reply_x.shape
    siblings = lax.axis_size("sibling")
    state = ssm_state.shape[3]
    widths = reply_query.shape[2]
    heads = a_log.shape[0]
    fork = fork_list.reshape(children)
    news = reply_kv.reshape(children, 2 * tokens, AHDIM)
    halves = state // 128
    bc = reply_bc.reshape(children, tokens, 2, halves, 128).transpose(0, 1, 3, 2, 4)
    bc = bc.reshape(children, tokens * 2 * halves, 128)
    pool = kv_pool.reshape(kv_pool.shape[0], 256, AHDIM)
    flat_state = ssm_state.reshape(channels, state)
    params = jnp.tile(jnp.stack([a_log, dt_bias, d_skip]), (1, 128 // heads))
    gain = norm_gain.reshape(1, channels)
    rows_bc = pltpu.VMEM((bc.shape[0] * bc.shape[1], 128), F32)

    sources = (bc, conv_x, conv_bc, fork, reply_query, news)
    fork_held = pltpu.SMEM(fork.shape, fork.dtype)
    held = [pltpu.VMEM(source.shape, source.dtype) for source in sources]
    held[3] = fork_held
    send = pl.pallas_call(
        pack_kernel,
        out_shape=jax.ShapeDtypeStruct((siblings, SEND_ROWS, 128), BF16),
        in_specs=[whole(pltpu.HBM)] * 6,
        out_specs=whole(),
        scratch_shapes=[pltpu.SMEM((siblings,), jnp.int32)]
        + held
        + [pltpu.SemaphoreType.DMA((6,)), rows_bc],
        **params_of(60, 1_000_000, 2_000_000),
    )(*sources)
    got = lax.all_to_all(send, "sibling", split_axis=0, concat_axis=0, tiled=True)

    pages = page_table.shape[1]
    prefix = pl.pallas_call(
        prefix_kernel,
        out_shape=jax.ShapeDtypeStruct((PREFIX_ARRAYS, pages * 128, AHDIM), BF16),
        grid_spec=pltpu.PrefetchScalarGridSpec(
            num_scalar_prefetch=1,
            grid=(pages,),
            in_specs=[pl.BlockSpec((1, 256, AHDIM), lambda i, table: (table[0, i], 0, 0))],
            out_specs=pl.BlockSpec((2, 128, AHDIM), lambda i, table: (0, i, 0)),
            scratch_shapes=[pltpu.VMEM((256, AHDIM), F32)],
        ),
        **params_of(60, 4_000_000, 8_000_000),
    )(page_table, pool)

    back, old_rows = pl.pallas_call(
        parent_kernel,
        out_shape=(
            jax.ShapeDtypeStruct((siblings, CAP, tokens, channels + widths), BF16),
            jax.ShapeDtypeStruct((HISTORY_ROOM, HIST_ROWS, 128), BF16),
        ),
        in_specs=[whole()] * 3 + [whole(pltpu.HBM)] * 2,
        out_specs=(whole(pltpu.HBM), whole(pltpu.HBM)),
        scratch_shapes=[
            pltpu.VMEM((pages * 128, AHDIM), BF16),
            pltpu.VMEM((pages * 128, 2 * AHDIM), BF16),
            pltpu.VMEM((channels, state), F32),
            pltpu.VMEM((siblings, CAP, tokens, channels), BF16),
            pltpu.VMEM((siblings // 2, 2, CAP, tokens, widths), BF16),
            pltpu.VMEM((siblings // 2, 64, AHDIM), F32),
            pltpu.SemaphoreType.DMA((3,)),
            pltpu.SemaphoreType.DMA((2 + siblings // 2,)),
        ],
        **params_of(50, 6_000_000_000, 8_000_000, 4_000_000),
    )(got, conv_bc, kernel_bc, prefix, flat_state)
    returned = lax.all_to_all(back, "sibling", split_axis=0, concat_axis=0, tiled=True)

    wide = jax.ShapeDtypeStruct((children, tokens, channels), F32)
    within, fade = pl.pallas_call(
        child_kernel,
        out_shape=(wide, jax.ShapeDtypeStruct((children * tokens, 128), BF16)),
        in_specs=[whole(pltpu.SMEM), whole(pltpu.HBM)] + [whole()] * 6,
        out_specs=(whole(), whole()),
        scratch_shapes=[
            pltpu.VMEM((siblings, HIST_ROWS, 128), BF16),
            pltpu.VMEM((children * tokens, channels + 2 * state), F32),
            pltpu.VMEM((8 * children * tokens, 128), BF16),
            rows_bc,
            pltpu.SemaphoreType.DMA,
        ],
        **params_of(44, 600_000_000, 8_000_000, 1_000_000),
    )(fork, old_rows, reply_x, bc, reply_dt, kernel_x, kernel_bc, params)

    mamba = jax.ShapeDtypeStruct((children, tokens, channels), BF16)
    attn = jax.ShapeDtypeStruct((children, tokens, widths), BF16)
    return pl.pallas_call(
        finish_kernel,
        out_shape=(mamba, attn),
        in_specs=[whole(pl.ANY)] * 2 + [whole()] * 5,
        out_specs=(whole(pltpu.HBM), whole(pltpu.HBM)),
        scratch_shapes=[
            pltpu.SMEM((siblings,), jnp.int32),
            fork_held,
            fork_held,
            pltpu.VMEM(wide.shape, F32),
            pltpu.VMEM(mamba.shape, BF16),
            pltpu.VMEM(attn.shape, BF16),
            pltpu.SemaphoreType.DMA((2,)),
            pltpu.SemaphoreType.DMA((2, 4)),
        ],
        **params_of(40, 10_000_000, 6_000_000),
    )(fork, lengths, returned, gain, fade, within, reply_gate)


def solution(mesh):
    return jax.shard_map(
        local,
        mesh=mesh,
        in_specs=(
            P(("replica", "sibling"), None, "tensor"),
            P(("replica", "sibling"), None, None, "tensor"),
            P(("replica", "sibling"), None, "tensor"),
            P(("replica", "sibling"), None, "tensor"),
            P(("replica", "sibling"), None, "tensor"),
            P(("replica", "sibling"), None, None, "tensor"),
            P(("replica", "sibling")),
            P(("replica", "sibling"), None),
            P(("replica", "sibling"), "tensor", None, None),
            P(("replica", "sibling"), None, "tensor"),
            P(("replica", "sibling"), None, None, "tensor"),
            P(("replica", "sibling"), None, None, "tensor"),
            P(("replica", "sibling"), None),
            P(None, "tensor"),
            P(None, None, "tensor"),
            P("tensor"),
            P("tensor"),
            P("tensor"),
            P("tensor"),
        ),
        out_specs=(
            P(("replica", "sibling"), None, "tensor"),
            P(("replica", "sibling"), None, "tensor"),
        ),
        check_vma=False,
    )
```

time: 81.3 us -> 67.2 us (0.83)
  Pallas kernels: 35.3 us -> 28 us
  local copies, waits for them, and re-layouts: 8.08 us -> 1.21 us
    pallas_call x4, Pallas kernels: 33.4 us -> 25.9 us  [the longest x1 9.74 us: local(): pl.pallas_call(prefix_kernel, out_shape=jax.ShapeDtypeStruct((PREFIX_ARRA...]
    unnamed x39 -> x26, local copies, waits for them, and re-layouts: 7.04 us -> 1.12 us
    all_to_all x1, waiting for transfers between devices: 15.8 us -> 17 us  [local(): lax.all_to_all(back, 'sibling', split_axis=0, concat_axis=0, tiled=True)]
    all_to_all x1, waiting for transfers between devices: 8.89 us -> 7.88 us  [local(): lax.all_to_all(send, 'sibling', split_axis=0, concat_axis=0, tiled=True)]
    reshape x1 -> x0, local copies, waits for them, and re-layouts: 0.96 us -> none  [local(): bc = reply_bc.reshape(children, 2 * tokens, state)]
  transfers between devices with their start and end apart: 2 -> 2, of which waited for: 2 -> 2; matrix products, arithmetic and copies ran while one was open for 0% -> 0% of each run, Pallas kernels for 19% -> 22%
where the time goes in v2:
time: 67.2 us; the launch traced here: 66.2 us
  Pallas kernels  28 us (42%)
  waiting for transfers between devices  24.9 us (37%)
  starting transfers between devices  11.1 us (17%)
  local copies, waits for them, and re-layouts  1.21 us (2%)
  between operations  0.99 us (1%)
    all_to_all x1, waiting for transfers between devices, local(): lax.all_to_all(back, 'sibling', split_axis=0, concat_axis=0, tiled=True)  17 us
    pallas_call x1, Pallas kernels, local(): pl.pallas_call(prefix_kernel, out_shape=jax.ShapeDtypeStruct((PREFIX_ARRA...  9.74 us
    pallas_call x1, Pallas kernels, local(): pl.pallas_call(parent_kernel, out_shape=(jax.ShapeDtypeStruct((siblings,...  9.1 us
    all_to_all x1, waiting for transfers between devices, local(): lax.all_to_all(send, 'sibling', split_axis=0, concat_axis=0, tiled=True)  7.88 us
    all_to_all x1, starting transfers between devices, local(): lax.all_to_all(send, 'sibling', split_axis=0, concat_axis=0, tiled=True)  7.05 us
    pallas_call x1, Pallas kernels, local(): pl.pallas_call(child_kernel, out_shape=(wide, jax.ShapeDtypeStruct((child...  4.91 us
    all_to_all x1, starting transfers between devices, local(): lax.all_to_all(back, 'sibling', split_axis=0, concat_axis=0, tiled=True)  4.03 us
    pallas_call x1, Pallas kernels, local(): pl.pallas_call(pack_kernel, out_shape=jax.ShapeDtypeStruct((siblings, SEN...  2.17 us
  transfers between devices with their start and end apart: 2, of which 2 were waited for; matrix products, arithmetic and copies ran while one was open for 0% of the time, Pallas kernels for 22%

profile of v2, /device:TPU:96, one launch (start us, length us, event | category | flops | bytes accessed | tf_op | source)
XLA Modules:
  0.0 66.2 jit_solution(16055063495328982317)
XLA Ops:
  0.6 2.2 %shard_map.194 = bf16[16,256,128]{2,1,0:T(8,128)(2,1)} custom-call(bf16[16,32,128]{2,1,0:T(8,128)(2,1)} %bitcast.13, bf16[1,3,2048]{2,1,0:T(4,128)(2,1)} %refs_1_.1, bf16[1,3,2,256]{3,2,1,0:T(2,128)(2,1)} %conv_bc.1, s32[16]{0:T(128)} %bitcast.16, bf16[16,8,1024]{2,1,0:T(8,128)(2,1)} %refs_4_.1, bf16[16,16,128]{2,1,0:T(8,128)(2,1)} %bitcast.20), custom_call_target="tpu_custom_call" | custom-call | flops 1000000 | bytes 2000000 | tf_op jit(solution)/shard_map/pallas_call | solution.py:384
  2.8 7.0 %all-to-all-start = ((bf16[16,256,128]{2,1,0:T(8,128)(2,1)}), bf16[16,256,128]{2,1,0:T(8,128)(2,1)S(1)}, u32[]{:S(2)}, u32[]{:S(2)}) async-start(bf16[16,256,128]{2,1,0:T(8,128)(2,1)} %shard_map.194), calls=%async_computation | async-start | bytes 2097152 | tf_op jit(solution)/shard_map/all_to_all | solution.py:394
  9.9 0.0 copy-start.5
  9.9 0.0 copy-start.8
  9.9 9.7 %shard_map.195.prefix_hbm = bf16[32,2048,128]{2,1,0:T(8,128)(2,1)} custom-call(s32[1,16]{1,0:T(1,128)} %table.1, bf16[32,256,128]{2,1,0:T(8,128)(2,1)} %bitcast.19), custom_call_target="tpu_custom_call" | custom-call | flops 4000000 | bytes 8000000 | tf_op jit(solution)/shard_map/pallas_call | solution.py:397
  19.6 7.9 %all-to-all-done.got = bf16[16,256,128]{2,1,0:T(8,128)(2,1)S(1)} async-done(((bf16[16,256,128]{2,1,0:T(8,128)(2,1)}), bf16[16,256,128]{2,1,0:T(8,128)(2,1)S(1)}, u32[]{:S(2)}, u32[]{:S(2)}) %all-to-all-start) | async-done | bytes 1048608 | tf_op jit(solution)/shard_map/all_to_all | solution.py:394
  27.5 0.0 copy-done.5
  27.5 0.0 copy-done.8
  27.5 9.1 %shard_map.196 = (bf16[16,2,8,3072]{3,2,1,0:T(8,128)(2,1)}, bf16[1024,64,128]{2,1,0:T(8,128)(2,1)}) custom-call(bf16[16,256,128]{2,1,0:T(8,128)(2,1)S(1)} %all-to-all-done.got, bf16[1,3,2,256]{3,2,1,0:T(2,128)(2,1)S(1)} %copy-done.8, f32[4,2,256]{2,1,0:T(2,128)S(1)} %copy-done.5, bf16[32,2048,128]{2,1,0:T(8,128)(2,1)} %shard_map.195.prefix_hbm, ...), custom_call_target="tpu_custom_call" | custom-call | flops 6000000000 | bytes 8000000 | tf_op jit(solution)/shard_map/pallas_call | solution.py:410
  36.6 0.0 copy-start.10
  36.6 0.0 copy-start.11
  36.6 0.0 copy-start.12
  36.6 0.0 copy-start
  36.7 0.0 copy-start.1
  36.7 0.0 copy-start.3
  36.7 0.0 copy-start.4
  36.7 0.0 copy-start.7
  36.7 4.0 %all-to-all-start.1 = ((bf16[16,2,8,3072]{3,2,1,0:T(8,128)(2,1)}), bf16[16,2,8,3072]{3,2,1,0:T(8,128)(2,1)S(1)}, u32[]{:S(2)}, u32[]{:S(2)}) async-start(bf16[16,2,8,3072]{3,2,1,0:T(8,128)(2,1)} %get-tuple-element.6), calls=%async_computation.1 | async-start | bytes 3145728 | tf_op jit(solution)/shard_map/all_to_all | solution.py:430
  40.7 0.0 copy-done.10
  40.8 0.0 copy-done.11
  40.8 0.0 copy-done.12
  40.8 0.1 tile.10.params
  40.9 0.0 copy-done
  40.9 0.0 copy-done.1
  40.9 0.0 copy-done.3
  40.9 0.0 copy-done.4
  40.9 0.0 copy-done.7
  40.9 0.0 copy-start.6
  40.9 0.0 copy-start.9
  40.9 4.9 %shard_map.197 = (f32[16,8,2048]{2,1,0:T(8,128)S(1)}, bf16[128,128]{1,0:T(8,128)(2,1)S(1)}) custom-call(s32[16]{0:T(128)S(1)} %bitcast.17, bf16[1024,64,128]{2,1,0:T(8,128)(2,1)} %get-tuple-element.7.old_rows_hbm, bf16[16,8,2048]{2,1,0:T(8,128)(2,1)S(1)} %copy-done.1, bf16[16,32,128]{2,1,0:T(8,128)(2,1)S(1)} %bitcast.14, bf16[16,8,32]{2,1,0:T(8,128)(2,1)S(1)} %copy-done.3, ...), custom_call_target="tpu_custom_call" | custom-call | flops 600000000 | bytes 8000000 | tf_op jit(solution)/shard_map/pallas_call | solution.py:433
  45.9 17.0 %all-to-all-done.1.got = bf16[16,2,8,3072]{3,2,1,0:T(8,128)(2,1)S(1)} async-done(((bf16[16,2,8,3072]{3,2,1,0:T(8,128)(2,1)}), bf16[16,2,8,3072]{3,2,1,0:T(8,128)(2,1)S(1)}, u32[]{:S(2)}, u32[]{:S(2)}) %all-to-all-start.1) | async-done | bytes 1572896 | tf_op jit(solution)/shard_map/all_to_all | solution.py:430
  62.9 0.0 copy-done.6
  62.9 0.0 copy-done.9
  62.9 0.0 copy-start.2
  62.9 1.0 %copy-done.2 = bf16[16,8,2048]{2,1,0:T(8,128)(2,1)S(1)} copy-done((bf16[16,8,2048]{2,1,0:T(8,128)(2,1)S(1)}, bf16[16,8,2048]{2,1,0:T(8,128)(2,1)}, u32[]{:S(2)}) %copy-start.2) | copy-done | bytes 524312
  63.9 2.1 %shard_map.198 = (bf16[16,8,2048]{2,1,0:T(8,128)(2,1)}, bf16[16,8,1024]{2,1,0:T(8,128)(2,1)}) custom-call(s32[16]{0:T(128)S(1)} %bitcast.18, s32[16]{0:T(128)S(1)} %copy-done.9, bf16[16,2,8,3072]{3,2,1,0:T(8,128)(2,1)S(1)} %all-to-all-done.1.got, f32[1,2048]{1,0:T(1,128)S(1)} %bitcast.15, bf16[128,128]{1,0:T(8,128)(2,1)S(1)} %get-tuple-element.8.fade, ...), custom_call_target="tpu_custom_call" | custom-call | flops 10000000 | bytes 6000000 | tf_op jit(solution)/shard_map/pallas_call | solution.py:450
  (2 shorter events, 0.0 us)
Async XLA Ops:
  2.8 24.7 %all-to-all-start = ((bf16[16,256,128]{2,1,0:T(8,128)(2,1)}), bf16[16,256,128]{2,1,0:T(8,128)(2,1)S(1)}, u32[]{:S(2)}, u32[]{:S(2)}) async-start(bf16[16,256,128]{2,1,0:T(8,128)(2,1)} %shard_map.194), calls=%async_computation | async-start | bytes 2097152 | tf_op jit(solution)/shard_map/all_to_all | solution.py:394
  9.9 17.6 %copy-start.5 = (f32[4,2,256]{2,1,0:T(2,128)S(1)}, f32[4,2,256]{2,1,0:T(2,128)}, u32[]{:S(2)}) copy-start(f32[4,2,256]{2,1,0:T(2,128)} %kernel_bc.3) | copy-start | bytes 24580
  9.9 17.6 %copy-start.8 = (bf16[1,3,2,256]{3,2,1,0:T(2,128)(2,1)S(1)}, bf16[1,3,2,256]{3,2,1,0:T(2,128)(2,1)}, u32[]{:S(2)}) copy-start(bf16[1,3,2,256]{3,2,1,0:T(2,128)(2,1)} %conv_bc.1) | copy-start | bytes 9220
  36.6 4.1 %copy-start.10 = (f32[32]{0:T(128)S(1)}, f32[32]{0:T(128)}, u32[]{:S(2)}) copy-start(f32[32]{0:T(128)} %param.36) | copy-start | bytes 388
  36.6 4.1 %copy-start.11 = (f32[32]{0:T(128)S(1)}, f32[32]{0:T(128)}, u32[]{:S(2)}) copy-start(f32[32]{0:T(128)} %param.35) | copy-start | bytes 388
  36.6 4.1 %copy-start.12 = (f32[32]{0:T(128)S(1)}, f32[32]{0:T(128)}, u32[]{:S(2)}) copy-start(f32[32]{0:T(128)} %param.34) | copy-start | bytes 388
  36.6 4.2 %copy-start = (bf16[16,8,2,256]{3,2,1,0:T(2,128)(2,1)S(1)}, bf16[16,8,2,256]{3,2,1,0:T(2,128)(2,1)}, u32[]{:S(2)}) copy-start(bf16[16,8,2,256]{3,2,1,0:T(2,128)(2,1)} %param.20) | copy-start | bytes 393220
  36.7 4.2 %copy-start.1 = (bf16[16,8,2048]{2,1,0:T(8,128)(2,1)S(1)}, bf16[16,8,2048]{2,1,0:T(8,128)(2,1)}, u32[]{:S(2)}) copy-start(bf16[16,8,2048]{2,1,0:T(8,128)(2,1)} %reply_x.1) | copy-start | bytes 1572868
  36.7 4.2 %copy-start.3 = (bf16[16,8,32]{2,1,0:T(8,128)(2,1)S(1)}, bf16[16,8,32]{2,1,0:T(8,128)(2,1)}, u32[]{:S(2)}) copy-start(bf16[16,8,32]{2,1,0:T(8,128)(2,1)} %dt.1) | copy-start | bytes 24580
  36.7 4.2 %copy-start.4 = (f32[4,2048]{1,0:T(4,128)S(1)}, f32[4,2048]{1,0:T(4,128)}, u32[]{:S(2)}) copy-start(f32[4,2048]{1,0:T(4,128)} %kernel_x.1) | copy-start | bytes 98308
  36.7 4.2 %copy-start.7 = (s32[16,1]{0,1:T(1,128)S(1)}, s32[16,1]{0,1:T(1,128)}, u32[]{:S(2)}) copy-start(s32[16,1]{0,1:T(1,128)} %param.26) | copy-start | bytes 196
  36.7 26.2 %all-to-all-start.1 = ((bf16[16,2,8,3072]{3,2,1,0:T(8,128)(2,1)}), bf16[16,2,8,3072]{3,2,1,0:T(8,128)(2,1)S(1)}, u32[]{:S(2)}, u32[]{:S(2)}) async-start(bf16[16,2,8,3072]{3,2,1,0:T(8,128)(2,1)} %get-tuple-element.6), calls=%async_computation.1 | async-start | bytes 3145728 | tf_op jit(solution)/shard_map/all_to_all | solution.py:430
  40.9 22.0 %copy-start.6 = (f32[2048]{0:T(1024)S(1)}, f32[2048]{0:T(1024)}, u32[]{:S(2)}) copy-start(f32[2048]{0:T(1024)} %param.37) | copy-start | bytes 24580
  40.9 22.0 %copy-start.9 = (s32[16]{0:T(128)S(1)}, s32[16]{0:T(128)}, u32[]{:S(2)}) copy-start(s32[16]{0:T(128)} %lengths_any.1) | copy-start | bytes 196
  62.9 1.0 %copy-start.2 = (bf16[16,8,2048]{2,1,0:T(8,128)(2,1)S(1)}, bf16[16,8,2048]{2,1,0:T(8,128)(2,1)}, u32[]{:S(2)}) copy-start(bf16[16,8,2048]{2,1,0:T(8,128)(2,1)} %gate.1) | copy-start | bytes 1572868

commit v3 on v2

--- a/solution.py
+++ b/solution.py
@@ -11,6 +11,7 @@
 CAP = 2
 PREFIX_ARRAYS = 32
 HISTORY_ROOM = 1024
+GATE_ROOM = 512
 NEGATIVE = -1e30
 EPSILON = 1e-05
 F32 = jnp.float32
@@ -142,10 +143,8 @@
     row_ids = lax.broadcasted_iota(jnp.int32, (256, 32), 0)
     col_ids = lax.broadcasted_iota(jnp.int32, (256, 32), 1)
     seen = jnp.logical_and(row_ids // 64 == col_ids // 8, row_ids % 8 >= col_ids % 8)
-    for load in loads[0:2]:
-        load.wait()
-
-    def attend(at):
+
+    def prepare(at):
         sender = 2 * at
         places = [(sender + i, slot * SLOT_ROWS) for i in range(2) for slot in range(CAP)]
         queries = jnp.concatenate([got[s, at : at + Q_ROWS, :] for s, at in places], axis=0)
@@ -156,11 +155,12 @@
         new_keys = mine[pl.ds(0, 32, stride=2), :].astype(BF16)
         new_values = mine[pl.ds(1, 32, stride=2), :].astype(BF16)
         new_values = jnp.concatenate([new_values, jnp.ones((32, 128), BF16)], axis=1)
+        reply = jnp.where(seen, transposed_dot(queries, new_keys), NEGATIVE)
+        return queries, reply, jnp.max(reply, axis=1, keepdims=True), new_values
+
+    def attend(at, queries, reply, reply_highest, new_values):
         scores = transposed_dot(queries, keys[...])
-        reply = jnp.where(seen, transposed_dot(queries, new_keys), NEGATIVE)
-        highest = jnp.maximum(
-            jnp.max(scores, axis=1, keepdims=True), jnp.max(reply, axis=1, keepdims=True)
-        )
+        highest = jnp.maximum(jnp.max(scores, axis=1, keepdims=True), reply_highest)
         weights = jnp.exp2((scores - highest) * factor).astype(BF16)
         reply_weights = jnp.exp2((reply - highest) * factor).astype(BF16)
         summed = jnp.dot(weights, values[...], preferred_element_type=F32)
@@ -176,8 +176,11 @@
         outs[-1].start()
 
     blocks = attn_rows.shape[0]
+    ready = [prepare(at) for at in range(blocks)]
+    for load in loads[0:2]:
+        load.wait()
     for at in range(blocks // 2):
-        attend(at)
+        attend(at, *ready[at])
     loads[2].wait()
     for at in range(0, channels, 256):
         part = state[at : at + 256, :]
@@ -192,7 +195,7 @@
     for at in range(blocks // 2):
         send_attended(at)
     for at in range(blocks // 2, blocks):
-        attend(at)
+        attend(at, *ready[at])
     for at in range(blocks // 2, blocks):
         send_attended(at)
     for copy in outs:
@@ -206,9 +209,11 @@
 
 
 def child_kernel(
-    fork, old_rows_hbm, reply_x, bc, dt, kernel_x, kernel_bc, params,
-    within, fade, old_rows, history, weights, rows_bc, sem,
+    fork, old_rows_hbm, reply_x, bc, dt, kernel_x, kernel_bc, params, gate,
+    within, fade, kept_gate, old_rows, history, weights, rows_bc, sem, sem_gate,
 ):
+    keep = pltpu.make_async_copy(gate, kept_gate.at[pl.ds(0, gate.shape[0])], sem_gate)
+    keep.start()
     load = pltpu.make_async_copy(old_rows_hbm.at[pl.ds(0, old_rows.shape[0])], old_rows, sem)
     load.start()
     load.wait()
@@ -288,15 +293,17 @@
             term = weight * xconv[:, source : source + 1, :]
             total = term if total is None else total + term
         within[:, :, at : at + per] = total
+    keep.wait()
 
 
 def finish_kernel(
-    fork_any, lengths_any, got, gain, fade, within, gate, mamba, attn,
-    count, fork, lengths, wide, mamba_rows, attn_rows, sems, sems_out,
+    fork_any, lengths_any, got, gain, fade, within, gate_hbm, mamba, attn,
+    count, fork, lengths, gate, wide, mamba_rows, attn_rows, sems, sems_out,
 ):
     loads = [
         pltpu.make_async_copy(fork_any, fork, sems.at[0]),
         pltpu.make_async_copy(lengths_any, lengths, sems.at[1]),
+        pltpu.make_async_copy(gate_hbm.at[pl.ds(0, gate.shape[0])], gate, sems.at[2]),
     ]
     for load in loads:
         load.start()
@@ -430,40 +437,46 @@
     returned = lax.all_to_all(back, "sibling", split_axis=0, concat_axis=0, tiled=True)
 
     wide = jax.ShapeDtypeStruct((children, tokens, channels), F32)
-    within, fade = pl.pallas_call(
+    within, fade, gate = pl.pallas_call(
         child_kernel,
-        out_shape=(wide, jax.ShapeDtypeStruct((children * tokens, 128), BF16)),
-        in_specs=[whole(pltpu.SMEM), whole(pltpu.HBM)] + [whole()] * 6,
-        out_specs=(whole(), whole()),
+        out_shape=(
+            wide,
+            jax.ShapeDtypeStruct((children * tokens, 128), BF16),
+            jax.ShapeDtypeStruct((GATE_ROOM,) + reply_gate.shape[1:], BF16),
+        ),
+        in_specs=[whole(pltpu.SMEM), whole(pltpu.HBM)] + [whole()] * 6 + [whole(pltpu.HBM)],
+        out_specs=(whole(), whole(), whole(pltpu.HBM)),
         scratch_shapes=[
             pltpu.VMEM((siblings, HIST_ROWS, 128), BF16),
             pltpu.VMEM((children * tokens, channels + 2 * state), F32),
             pltpu.VMEM((8 * children * tokens, 128), BF16),
             rows_bc,
             pltpu.SemaphoreType.DMA,
+            pltpu.SemaphoreType.DMA,
         ],
         **params_of(44, 600_000_000, 8_000_000, 1_000_000),
-    )(fork, old_rows, reply_x, bc, reply_dt, kernel_x, kernel_bc, params)
+    )(fork, old_rows, reply_x, bc, reply_dt, kernel_x, kernel_bc, params, reply_gate)
 
     mamba = jax.ShapeDtypeStruct((children, tokens, channels), BF16)
     attn = jax.ShapeDtypeStruct((children, tokens, widths), BF16)
     return pl.pallas_call(
         finish_kernel,
         out_shape=(mamba, attn),
-        in_specs=[whole(pl.ANY)] * 2 + [whole()] * 5,
+        in_specs=[whole(pl.ANY)] * 2 + [whole()] * 4 + [whole(pltpu.HBM)],
         out_specs=(whole(pltpu.HBM), whole(pltpu.HBM)),
         scratch_shapes=[
             pltpu.SMEM((siblings,), jnp.int32),
             fork_held,
             fork_held,
+            pltpu.VMEM(reply_gate.shape, BF16),
             pltpu.VMEM(wide.shape, F32),
             pltpu.VMEM(mamba.shape, BF16),
             pltpu.VMEM(attn.shape, BF16),
-            pltpu.SemaphoreType.DMA((2,)),
+            pltpu.SemaphoreType.DMA((3,)),
             pltpu.SemaphoreType.DMA((2, 4)),
         ],
-        **params_of(40, 10_000_000, 6_000_000),
-    )(fork, lengths, returned, gain, fade, within, reply_gate)
+        **params_of(46, 10_000_000, 6_000_000),
+    )(fork, lengths, returned, gain, fade, within, gate)
 
 
 def solution(mesh):

time: 67.2 us -> 66.7 us (level)
  waiting for transfers between devices: 24.9 us -> 23.7 us
  Pallas kernels: 28 us -> 28.7 us
    all_to_all x1, waiting for transfers between devices: 17 us -> 15.8 us  [local(): lax.all_to_all(back, 'sibling', split_axis=0, concat_axis=0, tiled=True)]
  transfers between devices with their start and end apart: 2 -> 2, of which waited for: 2 -> 2; matrix products, arithmetic and copies ran while one was open for 0% -> 0% of each run, Pallas kernels for 22% -> 23%
where the time goes in v3:
time: 66.7 us; the launch traced here: 65.7 us
  Pallas kernels  28.7 us (43%)
  waiting for transfers between devices  23.7 us (36%)
  starting transfers between devices  11.1 us (17%)
  local copies, waits for them, and re-layouts  1.19 us (2%)
  between operations  0.98 us (1%)
    all_to_all x1, waiting for transfers between devices, local(): lax.all_to_all(back, 'sibling', split_axis=0, concat_axis=0, tiled=True)  15.8 us
    pallas_call x1, Pallas kernels, local(): pl.pallas_call(prefix_kernel, out_shape=jax.ShapeDtypeStruct((PREFIX_ARRA...  9.74 us
    pallas_call x1, Pallas kernels, local(): pl.pallas_call(parent_kernel, out_shape=(jax.ShapeDtypeStruct((siblings,...  9.13 us
    all_to_all x1, waiting for transfers between devices, local(): lax.all_to_all(send, 'sibling', split_axis=0, concat_axis=0, tiled=True)  7.88 us
    all_to_all x1, starting transfers between devices, local(): lax.all_to_all(send, 'sibling', split_axis=0, concat_axis=0, tiled=True)  7.05 us
    pallas_call x1, Pallas kernels, local(): pl.pallas_call(child_kernel, out_shape=(wide, jax.ShapeDtypeStruct((child...  5.09 us
    all_to_all x1, starting transfers between devices, local(): lax.all_to_all(back, 'sibling', split_axis=0, concat_axis=0, tiled=True)  4.03 us
    pallas_call x1, Pallas kernels, local(): pl.pallas_call(finish_kernel, out_shape=(mamba, attn), in_specs=[whole(pl...  2.59 us
  transfers between devices with their start and end apart: 2, of which 2 were waited for; matrix products, arithmetic and copies ran while one was open for 0% of the time, Pallas kernels for 23%

profile of v3, /device:TPU:96, one launch (start us, length us, event | category | flops | bytes accessed | tf_op | source)
XLA Modules:
  0.0 65.7 jit_solution(1790288830490873664)
XLA Ops:
  0.6 2.2 %shard_map.194 = bf16[16,256,128]{2,1,0:T(8,128)(2,1)} custom-call(bf16[16,32,128]{2,1,0:T(8,128)(2,1)} %bitcast.13, bf16[1,3,2048]{2,1,0:T(4,128)(2,1)} %refs_1_.1, bf16[1,3,2,256]{3,2,1,0:T(2,128)(2,1)} %conv_bc.1, s32[16]{0:T(128)} %bitcast.16, bf16[16,8,1024]{2,1,0:T(8,128)(2,1)} %refs_4_.1, bf16[16,16,128]{2,1,0:T(8,128)(2,1)} %bitcast.20), custom_call_target="tpu_custom_call" | custom-call | flops 1000000 | bytes 2000000 | tf_op jit(solution)/shard_map/pallas_call | solution.py:391
  2.8 7.0 %all-to-all-start = ((bf16[16,256,128]{2,1,0:T(8,128)(2,1)}), bf16[16,256,128]{2,1,0:T(8,128)(2,1)S(1)}, u32[]{:S(2)}, u32[]{:S(2)}) async-start(bf16[16,256,128]{2,1,0:T(8,128)(2,1)} %shard_map.194), calls=%async_computation | async-start | bytes 2097152 | tf_op jit(solution)/shard_map/all_to_all | solution.py:401
  9.9 0.0 copy-start.5
  9.9 0.0 copy-start.8
  9.9 9.7 %shard_map.195.prefix_hbm = bf16[32,2048,128]{2,1,0:T(8,128)(2,1)} custom-call(s32[1,16]{1,0:T(1,128)} %table.1, bf16[32,256,128]{2,1,0:T(8,128)(2,1)} %bitcast.19), custom_call_target="tpu_custom_call" | custom-call | flops 4000000 | bytes 8000000 | tf_op jit(solution)/shard_map/pallas_call | solution.py:404
  19.6 7.9 %all-to-all-done.got = bf16[16,256,128]{2,1,0:T(8,128)(2,1)S(1)} async-done(((bf16[16,256,128]{2,1,0:T(8,128)(2,1)}), bf16[16,256,128]{2,1,0:T(8,128)(2,1)S(1)}, u32[]{:S(2)}, u32[]{:S(2)}) %all-to-all-start) | async-done | bytes 1048608 | tf_op jit(solution)/shard_map/all_to_all | solution.py:401
  27.5 0.0 copy-done.5
  27.5 0.0 copy-done.8
  27.5 9.1 %shard_map.196 = (bf16[16,2,8,3072]{3,2,1,0:T(8,128)(2,1)}, bf16[1024,64,128]{2,1,0:T(8,128)(2,1)}) custom-call(bf16[16,256,128]{2,1,0:T(8,128)(2,1)S(1)} %all-to-all-done.got, bf16[1,3,2,256]{3,2,1,0:T(2,128)(2,1)S(1)} %copy-done.8, f32[4,2,256]{2,1,0:T(2,128)S(1)} %copy-done.5, bf16[32,2048,128]{2,1,0:T(8,128)(2,1)} %shard_map.195.prefix_hbm, ...), custom_call_target="tpu_custom_call" | custom-call | flops 6000000000 | bytes 8000000 | tf_op jit(solution)/shard_map/pallas_call | solution.py:417
  36.6 0.0 copy-start.10
  36.7 0.0 copy-start.11
  36.7 0.0 copy-start.12
  36.7 0.0 copy-start
  36.7 0.0 copy-start.1
  36.7 0.0 copy-start.3
  36.7 0.0 copy-start.4
  36.7 0.0 copy-start.7
  36.7 4.0 %all-to-all-start.1 = ((bf16[16,2,8,3072]{3,2,1,0:T(8,128)(2,1)}), bf16[16,2,8,3072]{3,2,1,0:T(8,128)(2,1)S(1)}, u32[]{:S(2)}, u32[]{:S(2)}) async-start(bf16[16,2,8,3072]{3,2,1,0:T(8,128)(2,1)} %get-tuple-element.7), calls=%async_computation.1 | async-start | bytes 3145728 | tf_op jit(solution)/shard_map/all_to_all | solution.py:437
  40.8 0.0 copy-done.10
  40.8 0.0 copy-done.11
  40.8 0.0 copy-done.12
  40.8 0.1 tile.10.params
  40.9 0.0 copy-done
  40.9 0.0 copy-done.1
  40.9 0.0 copy-done.3
  40.9 0.0 copy-done.4
  40.9 0.0 copy-done.7
  41.0 0.0 copy-start.2
  41.0 1.0 %copy-done.2 = bf16[16,8,2048]{2,1,0:T(8,128)(2,1)S(1)} copy-done((bf16[16,8,2048]{2,1,0:T(8,128)(2,1)S(1)}, bf16[16,8,2048]{2,1,0:T(8,128)(2,1)}, u32[]{:S(2)}) %copy-start.2) | copy-done | bytes 524312
  42.0 0.0 copy-start.6
  42.0 0.0 copy-start.9
  42.0 5.1 %shard_map.197 = (f32[16,8,2048]{2,1,0:T(8,128)S(1)}, bf16[128,128]{1,0:T(8,128)(2,1)S(1)}, bf16[512,8,2048]{2,1,0:T(8,128)(2,1)}) custom-call(s32[16]{0:T(128)S(1)} %bitcast.17, bf16[1024,64,128]{2,1,0:T(8,128)(2,1)} %get-tuple-element.8.old_rows_hbm, bf16[16,8,2048]{2,1,0:T(8,128)(2,1)S(1)} %copy-done.1, bf16[16,32,128]{2,1,0:T(8,128)(2,1)S(1)} %bitcast.14, ...), custom_call_target="tpu_custom_call" | custom-call | flops 600000000 | bytes 8000000 | tf_op jit(solution)/shard_map/pallas_call | solution.py:440
  47.1 15.8 %all-to-all-done.1.got = bf16[16,2,8,3072]{3,2,1,0:T(8,128)(2,1)S(1)} async-done(((bf16[16,2,8,3072]{3,2,1,0:T(8,128)(2,1)}), bf16[16,2,8,3072]{3,2,1,0:T(8,128)(2,1)S(1)}, u32[]{:S(2)}, u32[]{:S(2)}) %all-to-all-start.1) | async-done | bytes 1572896 | tf_op jit(solution)/shard_map/all_to_all | solution.py:437
  62.9 0.0 copy-done.6
  62.9 0.0 copy-done.9
  62.9 2.6 %shard_map.198 = (bf16[16,8,2048]{2,1,0:T(8,128)(2,1)}, bf16[16,8,1024]{2,1,0:T(8,128)(2,1)}) custom-call(s32[16]{0:T(128)S(1)} %bitcast.18, s32[16]{0:T(128)S(1)} %copy-done.9, bf16[16,2,8,3072]{3,2,1,0:T(8,128)(2,1)S(1)} %all-to-all-done.1.got, f32[1,2048]{1,0:T(1,128)S(1)} %bitcast.15, bf16[128,128]{1,0:T(8,128)(2,1)S(1)} %get-tuple-element.9.fade, ...), custom_call_target="tpu_custom_call" | custom-call | flops 10000000 | bytes 6000000 | tf_op jit(solution)/shard_map/pallas_call | solution.py:462
  (2 shorter events, 0.0 us)
Async XLA Ops:
  2.8 24.7 %all-to-all-start = ((bf16[16,256,128]{2,1,0:T(8,128)(2,1)}), bf16[16,256,128]{2,1,0:T(8,128)(2,1)S(1)}, u32[]{:S(2)}, u32[]{:S(2)}) async-start(bf16[16,256,128]{2,1,0:T(8,128)(2,1)} %shard_map.194), calls=%async_computation | async-start | bytes 2097152 | tf_op jit(solution)/shard_map/all_to_all | solution.py:401
  9.9 17.6 %copy-start.5 = (f32[4,2,256]{2,1,0:T(2,128)S(1)}, f32[4,2,256]{2,1,0:T(2,128)}, u32[]{:S(2)}) copy-start(f32[4,2,256]{2,1,0:T(2,128)} %kernel_bc.3) | copy-start | bytes 24580
  9.9 17.6 %copy-start.8 = (bf16[1,3,2,256]{3,2,1,0:T(2,128)(2,1)S(1)}, bf16[1,3,2,256]{3,2,1,0:T(2,128)(2,1)}, u32[]{:S(2)}) copy-start(bf16[1,3,2,256]{3,2,1,0:T(2,128)(2,1)} %conv_bc.1) | copy-start | bytes 9220
  36.6 4.1 %copy-start.10 = (f32[32]{0:T(128)S(1)}, f32[32]{0:T(128)}, u32[]{:S(2)}) copy-start(f32[32]{0:T(128)} %param.36) | copy-start | bytes 388
  36.7 4.1 %copy-start.11 = (f32[32]{0:T(128)S(1)}, f32[32]{0:T(128)}, u32[]{:S(2)}) copy-start(f32[32]{0:T(128)} %param.35) | copy-start | bytes 388
  36.7 4.1 %copy-start.12 = (f32[32]{0:T(128)S(1)}, f32[32]{0:T(128)}, u32[]{:S(2)}) copy-start(f32[32]{0:T(128)} %param.34) | copy-start | bytes 388
  36.7 4.2 %copy-start = (bf16[16,8,2,256]{3,2,1,0:T(2,128)(2,1)S(1)}, bf16[16,8,2,256]{3,2,1,0:T(2,128)(2,1)}, u32[]{:S(2)}) copy-start(bf16[16,8,2,256]{3,2,1,0:T(2,128)(2,1)} %param.20) | copy-start | bytes 393220
  36.7 4.2 %copy-start.1 = (bf16[16,8,2048]{2,1,0:T(8,128)(2,1)S(1)}, bf16[16,8,2048]{2,1,0:T(8,128)(2,1)}, u32[]{:S(2)}) copy-start(bf16[16,8,2048]{2,1,0:T(8,128)(2,1)} %reply_x.1) | copy-start | bytes 1572868
  36.7 4.2 %copy-start.3 = (bf16[16,8,32]{2,1,0:T(8,128)(2,1)S(1)}, bf16[16,8,32]{2,1,0:T(8,128)(2,1)}, u32[]{:S(2)}) copy-start(bf16[16,8,32]{2,1,0:T(8,128)(2,1)} %dt.1) | copy-start | bytes 24580
  36.7 4.2 %copy-start.4 = (f32[4,2048]{1,0:T(4,128)S(1)}, f32[4,2048]{1,0:T(4,128)}, u32[]{:S(2)}) copy-start(f32[4,2048]{1,0:T(4,128)} %kernel_x.1) | copy-start | bytes 98308
  36.7 4.2 %copy-start.7 = (s32[16,1]{0,1:T(1,128)S(1)}, s32[16,1]{0,1:T(1,128)}, u32[]{:S(2)}) copy-start(s32[16,1]{0,1:T(1,128)} %param.26) | copy-start | bytes 196
  36.7 26.2 %all-to-all-start.1 = ((bf16[16,2,8,3072]{3,2,1,0:T(8,128)(2,1)}), bf16[16,2,8,3072]{3,2,1,0:T(8,128)(2,1)S(1)}, u32[]{:S(2)}, u32[]{:S(2)}) async-start(bf16[16,2,8,3072]{3,2,1,0:T(8,128)(2,1)} %get-tuple-element.7), calls=%async_computation.1 | async-start | bytes 3145728 | tf_op jit(solution)/shard_map/all_to_all | solution.py:437
  41.0 1.0 %copy-start.2 = (bf16[16,8,2048]{2,1,0:T(8,128)(2,1)S(1)}, bf16[16,8,2048]{2,1,0:T(8,128)(2,1)}, u32[]{:S(2)}) copy-start(bf16[16,8,2048]{2,1,0:T(8,128)(2,1)} %gate.1) | copy-start | bytes 1572868
  42.0 20.9 %copy-start.6 = (f32[2048]{0:T(1024)S(1)}, f32[2048]{0:T(1024)}, u32[]{:S(2)}) copy-start(f32[2048]{0:T(1024)} %param.37) | copy-start | bytes 24580
  42.0 20.9 %copy-start.9 = (s32[16]{0:T(128)S(1)}, s32[16]{0:T(128)}, u32[]{:S(2)}) copy-start(s32[16]{0:T(128)} %lengths_any.1) | copy-start | bytes 196

commit v4 on v3

--- a/solution.py
+++ b/solution.py
@@ -135,8 +135,7 @@
         joined = jnp.where(token < lag, early[None], moved).reshape(raw.shape)
         total = total + joined * taps[3 - lag]
     cmat = silu(total)
-    c_hi = cmat.astype(BF16)
-    c_lo = (cmat - c_hi.astype(F32)).astype(BF16)
+    cmat = cmat.astype(BF16)
     channels = state.shape[0]
 
     factor = AHDIM**-0.5 * math.log2(math.e)
@@ -183,10 +182,7 @@
         attend(at, *ready[at])
     loads[2].wait()
     for at in range(0, channels, 256):
-        part = state[at : at + 256, :]
-        high = part.astype(BF16)
-        low = (part - high.astype(F32)).astype(BF16)
-        read = transposed_dot(c_hi, high) + transposed_dot(c_lo, high) + transposed_dot(c_hi, low)
+        read = transposed_dot(cmat, state[at : at + 256, :].astype(BF16))
         read_rows[:, :, :, at : at + 256] = read.astype(BF16).reshape(senders, CAP, 8, 256)
     outs.append(
         pltpu.make_async_copy(read_rows, back.at[:, :, :, pl.ds(0, channels)], sems_out.at[1])

time: 66.7 us -> 66.2 us (level)
  no operation moved by 1% of the time
where the time goes in v4:
time: 66.2 us; the launch traced here: 65.1 us
  Pallas kernels  28.2 us (43%)
  waiting for transfers between devices  23.7 us (36%)
  starting transfers between devices  11.1 us (17%)
  local copies, waits for them, and re-layouts  1.19 us (2%)
  between operations  0.98 us (1%)
    all_to_all x1, waiting for transfers between devices, local(): lax.all_to_all(back, 'sibling', split_axis=0, concat_axis=0, tiled=True)  15.8 us
    pallas_call x1, Pallas kernels, local(): pl.pallas_call(prefix_kernel, out_shape=jax.ShapeDtypeStruct((PREFIX_ARRA...  9.74 us
    pallas_call x1, Pallas kernels, local(): pl.pallas_call(parent_kernel, out_shape=(jax.ShapeDtypeStruct((siblings,...  8.6 us
    all_to_all x1, waiting for transfers between devices, local(): lax.all_to_all(send, 'sibling', split_axis=0, concat_axis=0, tiled=True)  7.88 us
    all_to_all x1, starting transfers between devices, local(): lax.all_to_all(send, 'sibling', split_axis=0, concat_axis=0, tiled=True)  7.05 us
    pallas_call x1, Pallas kernels, local(): pl.pallas_call(child_kernel, out_shape=(wide, jax.ShapeDtypeStruct((child...  5.08 us
    all_to_all x1, starting transfers between devices, local(): lax.all_to_all(back, 'sibling', split_axis=0, concat_axis=0, tiled=True)  4.03 us
    pallas_call x1, Pallas kernels, local(): pl.pallas_call(finish_kernel, out_shape=(mamba, attn), in_specs=[whole(pl...  2.59 us
  transfers between devices with their start and end apart: 2, of which 2 were waited for; matrix products, arithmetic and copies ran while one was open for 0% of the time, Pallas kernels for 23%

profile of v4, /device:TPU:96, one launch (start us, length us, event | category | flops | bytes accessed | tf_op | source)
XLA Modules:
  0.0 65.1 jit_solution(9396543252931521971)
XLA Ops:
  0.6 2.2 %shard_map.194 = bf16[16,256,128]{2,1,0:T(8,128)(2,1)} custom-call(bf16[16,32,128]{2,1,0:T(8,128)(2,1)} %bitcast.13, bf16[1,3,2048]{2,1,0:T(4,128)(2,1)} %refs_1_.1, bf16[1,3,2,256]{3,2,1,0:T(2,128)(2,1)} %conv_bc.1, s32[16]{0:T(128)} %bitcast.16, bf16[16,8,1024]{2,1,0:T(8,128)(2,1)} %refs_4_.1, bf16[16,16,128]{2,1,0:T(8,128)(2,1)} %bitcast.20), custom_call_target="tpu_custom_call" | custom-call | flops 1000000 | bytes 2000000 | tf_op jit(solution)/shard_map/pallas_call | solution.py:387
  2.8 7.0 %all-to-all-start = ((bf16[16,256,128]{2,1,0:T(8,128)(2,1)}), bf16[16,256,128]{2,1,0:T(8,128)(2,1)S(1)}, u32[]{:S(2)}, u32[]{:S(2)}) async-start(bf16[16,256,128]{2,1,0:T(8,128)(2,1)} %shard_map.194), calls=%async_computation | async-start | bytes 2097152 | tf_op jit(solution)/shard_map/all_to_all | solution.py:397
  9.9 0.0 copy-start.5
  9.9 0.0 copy-start.8
  9.9 9.7 %shard_map.195.prefix_hbm = bf16[32,2048,128]{2,1,0:T(8,128)(2,1)} custom-call(s32[1,16]{1,0:T(1,128)} %table.1, bf16[32,256,128]{2,1,0:T(8,128)(2,1)} %bitcast.19), custom_call_target="tpu_custom_call" | custom-call | flops 4000000 | bytes 8000000 | tf_op jit(solution)/shard_map/pallas_call | solution.py:400
  19.6 7.9 %all-to-all-done.got = bf16[16,256,128]{2,1,0:T(8,128)(2,1)S(1)} async-done(((bf16[16,256,128]{2,1,0:T(8,128)(2,1)}), bf16[16,256,128]{2,1,0:T(8,128)(2,1)S(1)}, u32[]{:S(2)}, u32[]{:S(2)}) %all-to-all-start) | async-done | bytes 1048608 | tf_op jit(solution)/shard_map/all_to_all | solution.py:397
  27.5 0.0 copy-done.5
  27.5 0.0 copy-done.8
  27.5 8.6 %shard_map.196 = (bf16[16,2,8,3072]{3,2,1,0:T(8,128)(2,1)}, bf16[1024,64,128]{2,1,0:T(8,128)(2,1)}) custom-call(bf16[16,256,128]{2,1,0:T(8,128)(2,1)S(1)} %all-to-all-done.got, bf16[1,3,2,256]{3,2,1,0:T(2,128)(2,1)S(1)} %copy-done.8, f32[4,2,256]{2,1,0:T(2,128)S(1)} %copy-done.5, bf16[32,2048,128]{2,1,0:T(8,128)(2,1)} %shard_map.195.prefix_hbm, ...), custom_call_target="tpu_custom_call" | custom-call | flops 6000000000 | bytes 8000000 | tf_op jit(solution)/shard_map/pallas_call | solution.py:413
  36.1 0.0 copy-start.10
  36.1 0.0 copy-start.11
  36.1 0.0 copy-start.12
  36.2 0.0 copy-start
  36.2 0.0 copy-start.1
  36.2 0.0 copy-start.3
  36.2 0.0 copy-start.4
  36.2 0.0 copy-start.7
  36.2 4.0 %all-to-all-start.1 = ((bf16[16,2,8,3072]{3,2,1,0:T(8,128)(2,1)}), bf16[16,2,8,3072]{3,2,1,0:T(8,128)(2,1)S(1)}, u32[]{:S(2)}, u32[]{:S(2)}) async-start(bf16[16,2,8,3072]{3,2,1,0:T(8,128)(2,1)} %get-tuple-element.7), calls=%async_computation.1 | async-start | bytes 3145728 | tf_op jit(solution)/shard_map/all_to_all | solution.py:433
  40.3 0.0 copy-done.10
  40.3 0.0 copy-done.11
  40.3 0.0 copy-done.12
  40.3 0.1 tile.10.params
  40.4 0.0 copy-done
  40.4 0.0 copy-done.1
  40.4 0.0 copy-done.3
  40.4 0.0 copy-done.4
  40.4 0.0 copy-done.7
  40.4 0.0 copy-start.2
  40.4 1.0 %copy-done.2 = bf16[16,8,2048]{2,1,0:T(8,128)(2,1)S(1)} copy-done((bf16[16,8,2048]{2,1,0:T(8,128)(2,1)S(1)}, bf16[16,8,2048]{2,1,0:T(8,128)(2,1)}, u32[]{:S(2)}) %copy-start.2) | copy-done | bytes 524312
  41.5 0.0 copy-start.6
  41.5 0.0 copy-start.9
  41.5 5.1 %shard_map.197 = (f32[16,8,2048]{2,1,0:T(8,128)S(1)}, bf16[128,128]{1,0:T(8,128)(2,1)S(1)}, bf16[512,8,2048]{2,1,0:T(8,128)(2,1)}) custom-call(s32[16]{0:T(128)S(1)} %bitcast.17, bf16[1024,64,128]{2,1,0:T(8,128)(2,1)} %get-tuple-element.8.old_rows_hbm, bf16[16,8,2048]{2,1,0:T(8,128)(2,1)S(1)} %copy-done.1, bf16[16,32,128]{2,1,0:T(8,128)(2,1)S(1)} %bitcast.14, ...), custom_call_target="tpu_custom_call" | custom-call | flops 600000000 | bytes 8000000 | tf_op jit(solution)/shard_map/pallas_call | solution.py:436
  46.6 15.8 %all-to-all-done.1.got = bf16[16,2,8,3072]{3,2,1,0:T(8,128)(2,1)S(1)} async-done(((bf16[16,2,8,3072]{3,2,1,0:T(8,128)(2,1)}), bf16[16,2,8,3072]{3,2,1,0:T(8,128)(2,1)S(1)}, u32[]{:S(2)}, u32[]{:S(2)}) %all-to-all-start.1) | async-done | bytes 1572896 | tf_op jit(solution)/shard_map/all_to_all | solution.py:433
  62.4 0.0 copy-done.6
  62.4 0.0 copy-done.9
  62.4 2.6 %shard_map.198 = (bf16[16,8,2048]{2,1,0:T(8,128)(2,1)}, bf16[16,8,1024]{2,1,0:T(8,128)(2,1)}) custom-call(s32[16]{0:T(128)S(1)} %bitcast.18, s32[16]{0:T(128)S(1)} %copy-done.9, bf16[16,2,8,3072]{3,2,1,0:T(8,128)(2,1)S(1)} %all-to-all-done.1.got, f32[1,2048]{1,0:T(1,128)S(1)} %bitcast.15, bf16[128,128]{1,0:T(8,128)(2,1)S(1)} %get-tuple-element.9.fade, ...), custom_call_target="tpu_custom_call" | custom-call | flops 10000000 | bytes 6000000 | tf_op jit(solution)/shard_map/pallas_call | solution.py:458
  (2 shorter events, 0.0 us)
Async XLA Ops:
  2.8 24.7 %all-to-all-start = ((bf16[16,256,128]{2,1,0:T(8,128)(2,1)}), bf16[16,256,128]{2,1,0:T(8,128)(2,1)S(1)}, u32[]{:S(2)}, u32[]{:S(2)}) async-start(bf16[16,256,128]{2,1,0:T(8,128)(2,1)} %shard_map.194), calls=%async_computation | async-start | bytes 2097152 | tf_op jit(solution)/shard_map/all_to_all | solution.py:397
  9.9 17.6 %copy-start.5 = (f32[4,2,256]{2,1,0:T(2,128)S(1)}, f32[4,2,256]{2,1,0:T(2,128)}, u32[]{:S(2)}) copy-start(f32[4,2,256]{2,1,0:T(2,128)} %kernel_bc.3) | copy-start | bytes 24580
  9.9 17.6 %copy-start.8 = (bf16[1,3,2,256]{3,2,1,0:T(2,128)(2,1)S(1)}, bf16[1,3,2,256]{3,2,1,0:T(2,128)(2,1)}, u32[]{:S(2)}) copy-start(bf16[1,3,2,256]{3,2,1,0:T(2,128)(2,1)} %conv_bc.1) | copy-start | bytes 9220
  36.1 4.1 %copy-start.10 = (f32[32]{0:T(128)S(1)}, f32[32]{0:T(128)}, u32[]{:S(2)}) copy-start(f32[32]{0:T(128)} %param.36) | copy-start | bytes 388
  36.1 4.1 %copy-start.11 = (f32[32]{0:T(128)S(1)}, f32[32]{0:T(128)}, u32[]{:S(2)}) copy-start(f32[32]{0:T(128)} %param.35) | copy-start | bytes 388
  36.1 4.1 %copy-start.12 = (f32[32]{0:T(128)S(1)}, f32[32]{0:T(128)}, u32[]{:S(2)}) copy-start(f32[32]{0:T(128)} %param.34) | copy-start | bytes 388
  36.2 4.2 %copy-start = (bf16[16,8,2,256]{3,2,1,0:T(2,128)(2,1)S(1)}, bf16[16,8,2,256]{3,2,1,0:T(2,128)(2,1)}, u32[]{:S(2)}) copy-start(bf16[16,8,2,256]{3,2,1,0:T(2,128)(2,1)} %param.20) | copy-start | bytes 393220
  36.2 4.2 %copy-start.1 = (bf16[16,8,2048]{2,1,0:T(8,128)(2,1)S(1)}, bf16[16,8,2048]{2,1,0:T(8,128)(2,1)}, u32[]{:S(2)}) copy-start(bf16[16,8,2048]{2,1,0:T(8,128)(2,1)} %reply_x.1) | copy-start | bytes 1572868
  36.2 4.2 %copy-start.3 = (bf16[16,8,32]{2,1,0:T(8,128)(2,1)S(1)}, bf16[16,8,32]{2,1,0:T(8,128)(2,1)}, u32[]{:S(2)}) copy-start(bf16[16,8,32]{2,1,0:T(8,128)(2,1)} %dt.1) | copy-start | bytes 24580
  36.2 4.2 %copy-start.4 = (f32[4,2048]{1,0:T(4,128)S(1)}, f32[4,2048]{1,0:T(4,128)}, u32[]{:S(2)}) copy-start(f32[4,2048]{1,0:T(4,128)} %kernel_x.1) | copy-start | bytes 98308
  36.2 4.2 %copy-start.7 = (s32[16,1]{0,1:T(1,128)S(1)}, s32[16,1]{0,1:T(1,128)}, u32[]{:S(2)}) copy-start(s32[16,1]{0,1:T(1,128)} %param.26) | copy-start | bytes 196
  36.2 26.2 %all-to-all-start.1 = ((bf16[16,2,8,3072]{3,2,1,0:T(8,128)(2,1)}), bf16[16,2,8,3072]{3,2,1,0:T(8,128)(2,1)S(1)}, u32[]{:S(2)}, u32[]{:S(2)}) async-start(bf16[16,2,8,3072]{3,2,1,0:T(8,128)(2,1)} %get-tuple-element.7), calls=%async_computation.1 | async-start | bytes 3145728 | tf_op jit(solution)/shard_map/all_to_all | solution.py:433
  40.4 1.0 %copy-start.2 = (bf16[16,8,2048]{2,1,0:T(8,128)(2,1)S(1)}, bf16[16,8,2048]{2,1,0:T(8,128)(2,1)}, u32[]{:S(2)}) copy-start(bf16[16,8,2048]{2,1,0:T(8,128)(2,1)} %gate.1) | copy-start | bytes 1572868
  41.5 20.9 %copy-start.6 = (f32[2048]{0:T(1024)S(1)}, f32[2048]{0:T(1024)}, u32[]{:S(2)}) copy-start(f32[2048]{0:T(1024)} %param.37) | copy-start | bytes 24580
  41.5 20.9 %copy-start.9 = (s32[16]{0:T(128)S(1)}, s32[16]{0:T(128)}, u32[]{:S(2)}) copy-start(s32[16]{0:T(128)} %lengths_any.1) | copy-start | bytes 196
